TPU v7x, 32 devices: a whole 2x2x4 slice. The times are simulated.
32 devices in a mesh: ens: 2 (over x), lon: 16 (over z, y, core).
Axes of the slice: x: 2, y: 2, z: 4, core: 2. Of those that a mesh axis runs over, the one named last changes fastest.
Arguments:
- activations: bfloat16 [128, 768, 256], P('ens', 'lon'), parts along dimension 0, may hold values from -6 to 6
- quadrature: bfloat16 [4, 64, 3, 16], replicated, may hold values from -1.5 to 1.5
- support: int32 [4, 16], replicated, may hold values from -24 to 24, as said below
- support_count: int32 [4], replicated, may hold values from 2 to 16, as said below
- weight_first: bfloat16 [4, 256, 256], replicated, may hold values from -0.1875 to 0.1875
- weight_second: bfloat16 [4, 256, 256], replicated, may hold values from -0.1875 to 0.1875
- cotangent: bfloat16 [128, 768, 256], P('ens', 'lon'), parts along dimension 0, may hold values from -6 to 6
Outputs:
- mixed: bfloat16 [128, 768, 256], P('ens', 'lon'), parts along dimension 0
- grad_field: bfloat16 [128, 768, 256], P('ens', 'lon'), parts along dimension 0
- grad_first: float32 [8, 256, 256], P('ens'), parts along dimension 0
- grad_second: float32 [8, 256, 256], P('ens'), parts along dimension 0
There are 2 independent parts, one for each index of `ens`. A program takes and returns all parts, laid end to end along the dimension named above; an argument that names none is the same for every part. Nothing has to cross between parts.
Inputs may be any that keep to these rules, and one draw needn't show every extreme that they name: In band b the first support_count[b] entries of support[b] are distinct, lie within -reach(b) .. reach(b), and include both -reach(b) and reach(b); the remaining entries are padding. `support_count`: for band b at most min(16, 2 reach(b) + 1); the last band's count is 16.
All inputs are finite; a program needn't handle non-finite values.
Results may differ from a plain program's by a relative error of at most 0.015.
Values may be sent and summed in bfloat16 or wider, within the bound.
A program may use at most 192 MiB of HBM per device.

v0:
```python
import functools
import math

import jax
import jax.numpy as jnp
from jax import lax
from jax.experimental import pallas as pl
from jax.experimental.pallas import tpu as pltpu
from jax.sharding import PartitionSpec as P

LANES = 128
VMEM_LIMIT = 56 * 1024 * 1024


def gelu_cdf(value):
    return 0.5 + 0.5 * lax.erf(value * 0.7071067811865476)


def gelu_slope(value):
    density = jnp.exp(-0.5 * value * value) * 0.3989422804014327
    return gelu_cdf(value) + value * density


def tap_tables(quadrature, support, support_count, halo):
    kernel_count, rows, taps, slots = quadrature.shape
    bands = support.shape[0]
    band_rows = rows // bands
    live = lax.broadcasted_iota(jnp.int32, support.shape, 1) < support_count[:, None]
    lane = jnp.arange(LANES, dtype=jnp.int32)
    by_band = quadrature.reshape(kernel_count, bands, band_rows, taps, slots)

    def place(sign):
        hot = ((halo + sign * support)[:, :, None] == lane) & live[:, :, None]
        table = jnp.einsum(
            "kbrds,bsl->brkdl", by_band, hot.astype(jnp.bfloat16), preferred_element_type=jnp.float32
        )
        return table.reshape(rows, kernel_count, taps, LANES)

    row = jnp.arange(rows)[:, None, None, None]
    tap = jnp.arange(taps)[None, None, :, None]
    inside = (row + tap >= 1) & (row + tap <= rows)
    ahead = jnp.where(inside, place(1), 0.0)
    source = jnp.pad(place(-1), ((1, 1), (0, 0), (0, 0), (0, 0)))
    back = jnp.stack([source[e : e + rows, :, taps - 1 - e] for e in range(taps)], 2)
    shape = (rows, kernel_count * taps, LANES)
    return ahead.reshape(shape), back.reshape(shape)


def fill_matrices(table_ref, matrix_ref, row, cols):
    table = table_ref[row]
    for k in range(table.shape[0] // 3):
        for d in range(3):
            line = jnp.broadcast_to(table[k * 3 + d][None], (cols, LANES))
            rolled = pltpu.roll(line, 0, 1, stride=1, stride_axis=0)
            matrix_ref[row, k * cols : (k + 1) * cols, d * LANES : (d + 1) * LANES] = rolled.astype(
                jnp.bfloat16
            )


def spread_block(own, low, high, matrix, matrix_row, spread, first_row, count):
    rows, cols, channels = own.shape
    filler = jnp.zeros((LANES - cols - 2 * low.shape[1], channels), jnp.bfloat16)
    for r in range(count):
        parts = []
        for d in range(3):
            src = jnp.clip(first_row + r + d - 1, 0, rows - 1)
            parts += [low[src], own[src], high[src], filler]
        mixed = jnp.dot(
            matrix[matrix_row + r],
            jnp.concatenate(parts, 0),
            preferred_element_type=jnp.float32,
        ).astype(jnp.bfloat16)
        for k in range(mixed.shape[0] // cols):
            spread[r * cols : (r + 1) * cols, k * channels : (k + 1) * channels] = mixed[
                k * cols : (k + 1) * cols
            ]


def matrices_kernel(block, cols, ahead_ref, back_ref, ahead_out, back_out):
    def body(row, carry):
        fill_matrices(ahead_ref, ahead_out, row, cols)
        fill_matrices(back_ref, back_out, row, cols)
        return carry

    lax.fori_loop(0, block, body, 0)


def add_outer(left, spread, grad_ref, step):
    part = lax.dot_general(
        left, spread, (((0,), (0,)), ((), ())), preferred_element_type=jnp.float32
    )

    @pl.when(step == 0)
    def _():
        grad_ref[...] = part

    @pl.when(step > 0)
    def _():
        grad_ref[...] += part


def first_kernel(block, own, low, high, matrix, weight, pre_out, act_out, spread_out):
    step = pl.program_id(0)
    spread_block(own, low, high, matrix, 0, spread_out, step * block, block)
    pre = jnp.dot(spread_out[...], weight[...], preferred_element_type=jnp.float32)
    pre_out[...] = pre
    act_out[...] = (pre * gelu_cdf(pre)).astype(jnp.bfloat16).reshape(act_out.shape)


def slope_kernel(
    block, scale, own, low, high, matrix, weight, pre, spread_one, gp_out, grad_out, spread, grad
):
    step = pl.program_id(0)
    spread_block(own, low, high, matrix, 0, spread, step * block, block)
    grad_act = jnp.dot(spread[...], weight[...], preferred_element_type=jnp.float32)
    gp = (grad_act * gelu_slope(pre[...])).astype(jnp.bfloat16)
    gp_out[...] = gp.reshape(gp_out.shape)
    add_outer(gp, spread_one[...], grad, step)

    @pl.when(step == pl.num_programs(0) - 1)
    def _():
        grad_out[...] = (grad[...] * scale).T.astype(jnp.bfloat16)


def second_kernel(
    block, scale, own, low, high, matrix, weight, resid, cot, mixed_out, grad_out, spread, grad
):
    step = pl.program_id(0)
    spread_block(own, low, high, matrix, 0, spread, step * block, block)
    branch = jnp.dot(spread[...], weight[...], preferred_element_type=jnp.float32)
    flat = branch.shape
    mixed_out[...] = (
        (resid[...].reshape(flat).astype(jnp.float32) + branch)
        .astype(jnp.bfloat16)
        .reshape(mixed_out.shape)
    )
    add_outer(cot[...].reshape(flat), spread[...], grad, step)

    @pl.when(step == pl.num_programs(0) - 1)
    def _():
        grad_out[...] = (grad[...] * scale).T.astype(jnp.bfloat16)


def last_kernel(block, own, low, high, matrix, weight, cot, field_out, spread):
    step = pl.program_id(0)
    spread_block(own, low, high, matrix, 0, spread, step * block, block)
    adj = jnp.dot(spread[...], weight[...], preferred_element_type=jnp.float32)
    field_out[...] = (
        (cot[...].reshape(adj.shape).astype(jnp.float32) + adj)
        .astype(jnp.bfloat16)
        .reshape(field_out.shape)
    )


def halos(field, halo):
    count = lax.axis_size("lon")
    cols = field.shape[1]
    forward = [(i, (i + 1) % count) for i in range(count)]
    backward = [(target, source) for source, target in forward]
    low = lax.ppermute(field[:, cols - halo :], "lon", forward)
    high = lax.ppermute(field[:, :halo], "lon", backward)
    return low, high


def on_device(
    activations, quadrature, support, support_count, weight_first, weight_second, cotangent
):
    rows, cols, channels = activations.shape
    kernels = weight_first.shape[0]
    halo = -(-(cols // 2) // 16) * 16
    block = 8
    steps = rows // block
    wide = kernels * channels
    scale = 1.0 / math.sqrt(rows * cols * lax.axis_size("lon"))
    flat_first = weight_first.reshape(wide, channels)
    flat_second = weight_second.reshape(wide, channels)
    turned_first = weight_first.swapaxes(1, 2).reshape(wide, channels)
    turned_second = weight_second.swapaxes(1, 2).reshape(wide, channels)
    ahead, back = tap_tables(quadrature, support, support_count, halo)

    params = pltpu.CompilerParams(vmem_limit_bytes=VMEM_LIMIT)
    bf16, f32 = jnp.bfloat16, jnp.float32
    whole = lambda shape: pl.BlockSpec(shape, lambda i: (0,) * len(shape))
    by_row = lambda shape: pl.BlockSpec(shape, lambda i: (i,) + (0,) * (len(shape) - 1))
    field_spec = by_row((block, cols, channels))
    matrix_spec = by_row((block, kernels * cols, 3 * LANES))
    common = [
        whole((rows, cols, channels)),
        whole((rows, halo, channels)),
        whole((rows, halo, channels)),
        matrix_spec,
        whole((wide, channels)),
    ]
    spread_shape = (block * cols, wide)
    field_type = jax.ShapeDtypeStruct((rows, cols, channels), bf16)
    grad_type = jax.ShapeDtypeStruct((wide, channels), bf16)
    work = [pltpu.VMEM(spread_shape, bf16), pltpu.VMEM((channels, wide), f32)]
    cost = pl.CostEstimate(flops=6 * 10**9, bytes_accessed=20 * 10**6, transcendentals=0)

    def call(body, **kw):
        return pl.pallas_call(
            body, grid=(steps,), compiler_params=params, cost_estimate=cost, **kw
        )

    matrix_type = jax.ShapeDtypeStruct((rows, kernels * cols, 3 * LANES), bf16)
    act_low, act_high = halos(activations, halo)
    cot_low, cot_high = halos(cotangent, halo)
    table_spec = by_row((block, kernels * 3, LANES))
    m_ahead, m_back = call(
        functools.partial(matrices_kernel, block, cols),
        in_specs=[table_spec, table_spec],
        out_specs=[matrix_spec, matrix_spec],
        out_shape=[matrix_type, matrix_type],
    )(ahead, back)
    cells = rows * cols
    pre, activated, spread_one = call(
        functools.partial(first_kernel, block),
        in_specs=common,
        out_specs=[by_row((block * cols, channels)), field_spec, by_row(spread_shape)],
        out_shape=[
            jax.ShapeDtypeStruct((cells, channels), f32),
            field_type,
            jax.ShapeDtypeStruct((cells, wide), bf16),
        ],
    )(activations, act_low, act_high, m_ahead, flat_first)
    mid_low, mid_high = halos(activated, halo)
    gp, grad_first = call(
        functools.partial(slope_kernel, block, scale),
        in_specs=common + [by_row((block * cols, channels)), by_row(spread_shape)],
        out_specs=[field_spec, whole((wide, channels))],
        out_shape=[field_type, grad_type],
        scratch_shapes=work,
    )(cotangent, cot_low, cot_high, m_back, turned_second, pre, spread_one)
    gp_low, gp_high = halos(gp, halo)
    total_first = lax.psum(grad_first, "lon")
    mixed, grad_second = call(
        functools.partial(second_kernel, block, scale),
        in_specs=common + [field_spec, field_spec],
        out_specs=[field_spec, whole((wide, channels))],
        out_shape=[field_type, grad_type],
        scratch_shapes=work,
    )(activated, mid_low, mid_high, m_ahead, flat_second, activations, cotangent)
    total_second = lax.psum(grad_second, "lon")
    grad_field = call(
        functools.partial(last_kernel, block),
        in_specs=common + [field_spec],
        out_specs=field_spec,
        out_shape=field_type,
        scratch_shapes=work[:1],
    )(gp, gp_low, gp_high, m_back, turned_first, cotangent)
    return (
        mixed,
        grad_field,
        total_first.astype(f32).reshape(kernels, channels, channels),
        total_second.astype(f32).reshape(kernels, channels, channels),
    )


def solution(mesh):
    placed = (P("ens", "lon", None), P(), P(), P(), P(), P(), P("ens", "lon", None))
    return jax.shard_map(
        on_device,
        mesh=mesh,
        in_specs=placed,
        out_specs=(
            P("ens", "lon", None),
            P("ens", "lon", None),
            P("ens", None, None),
            P("ens", None, None),
        ),
        check_vma=False,
    )
```

profile of v0, /device:TPU:0, one launch (start us, length us, event | category | flops | bytes accessed | tf_op | source)
XLA Modules:
  0.0 213.0 jit_solution(12494489462472773888)
XLA Ops:
  7.2 0.0 copy-start
  7.2 0.0 all-reduce.4.cloned.1.call-start
  7.2 3.2 %fusion.16 = (bf16[64,32,256]{2,1,0:T(8,128)(2,1)}, bf16[64,32,256]{2,1,0:T(8,128)(2,1)}) fusion(bf16[64,48,256]{2,1,0:T(8,128)(2,1)} %resid.1), kind=kLoop, calls=%fused_computation.26 | loop fusion | bytes 4194304 | tf_op jit(solution)/shard_map/slice | solution.py:161
  10.4 0.5 collective-permute-start
  10.8 5.1 %collective-permute-start.1 = (bf16[64,32,256]{2,1,0:T(8,128)(2,1)}, bf16[64,32,256]{2,1,0:T(8,128)(2,1)}, u32[]{:S(2)}, u32[]{:S(2)}) collective-permute-start(bf16[64,32,256]{2,1,0:T(8,128)(2,1)} %get-tuple-element.30), channel_id=1, source_target_pairs={{1,0},{2,1},{3,2},{4,3},{5,4},{6,5},{7,6},{8,7},{9,8},{10,9},{11,1... | collective-permute-start | bytes 3145736 | tf_op jit(solution)/shard_map/ppermute | solution.py:161
  15.9 0.0 copy-done
  15.9 1.3 fusion.14
  17.2 0.0 collective-permute-start.4
  17.2 4.4 %collective-permute-start.5 = (bf16[64,32,256]{2,1,0:T(8,128)(2,1)S(1)}, bf16[64,32,256]{2,1,0:T(8,128)(2,1)S(1)}, u32[]{:S(2)}, u32[]{:S(2)}) collective-permute-start(bf16[64,32,256]{2,1,0:T(8,128)(2,1)S(1)} %get-tuple-element.26), channel_id=1, source_target_pairs={{1,0},{2,1},{3,2},{4,3},{5,4},{6,5},{7,6},{8,7},{9,8},{10,9},{11,1... | collective-permute-start | bytes 3145736 | tf_op jit(solution)/shard_map/ppermute | solution.py:161
  21.6 0.0 copy-done.5
  21.6 0.1 reshape.89
  21.8 0.2 copy.17
  22.0 0.0 copy-done.6
  22.0 0.0 copy-done.7
  22.0 0.1 iota_compare_fusion.2
  22.1 0.3 convolution_bitcast_fusion
  22.4 1.1 copy.22.back_ref
  23.5 0.3 convolution_bitcast_fusion.1
  23.8 0.1 copy.16
  24.0 1.1 copy_select_fusion.ahead_ref
  25.1 12.5 %shard_map.102 = (bf16[64,192,384]{2,1,0:T(8,128)(2,1)}, bf16[64,192,384]{2,1,0:T(8,128)(2,1)}) custom-call(f32[64,12,128]{2,1,0:T(8,128)} %copy_select_fusion.ahead_ref, f32[64,12,128]{2,1,0:T(8,128)} %copy.22.back_ref), custom_call_target="tpu_custom_call" | custom-call | flops 6000000000 | bytes 20000000 | tf_op jit(solution)/shard_map/pallas_call | solution.py:209
  37.6 2.1 copy.23
  39.7 0.0 collective-permute-done.low
  39.7 0.0 collective-permute-done.1.high
  39.7 13.3 %shard_map.103 = (f32[3072,256]{1,0:T(8,128)}, bf16[64,48,256]{2,1,0:T(8,128)(2,1)}, bf16[3072,1024]{1,0:T(8,128)(2,1)}) custom-call(bf16[64,48,256]{2,1,0:T(8,128)(2,1)} %resid.1, bf16[64,32,256]{2,1,0:T(8,128)(2,1)} %collective-permute-done.low, bf16[64,32,256]{2,1,0:T(8,128)(2,1)} %collective-permute-done.1.high, ...), custom_call_target="tpu_custom_call" | custom-call | flops 6000000000 | bytes 20000000 | tf_op jit(solution)/shard_map/pallas_call | solution.py:216
  53.0 3.0 %fusion.15 = (bf16[64,32,256]{2,1,0:T(8,128)(2,1)}, bf16[64,32,256]{2,1,0:T(8,128)(2,1)}) fusion(bf16[64,48,256]{2,1,0:T(8,128)(2,1)} %get-tuple-element.14.own), kind=kLoop, calls=%fused_computation.25 | loop fusion | bytes 4194304 | tf_op jit(solution)/shard_map/slice | solution.py:161
  56.1 10.8 %collective-permute-start.2 = (bf16[64,32,256]{2,1,0:T(8,128)(2,1)}, bf16[64,32,256]{2,1,0:T(8,128)(2,1)}, u32[]{:S(2)}, u32[]{:S(2)}) collective-permute-start(bf16[64,32,256]{2,1,0:T(8,128)(2,1)} %get-tuple-element.29), channel_id=1, source_target_pairs={{0,1},{1,2},{2,3},{3,4},{4,5},{5,6},{6,7},{7,8},{8,9},{9,10},{10,1... | collective-permute-start | bytes 3145736 | tf_op jit(solution)/shard_map/ppermute | solution.py:160
  66.8 0.0 collective-permute-start.3
  66.8 0.0 collective-permute-done.4.low
  66.9 0.0 collective-permute-done.5.high
  66.9 0.0 copy-start.2
  66.9 0.9 copy-done.1
  67.8 0.4 copy-done.2
  68.2 17.7 %shard_map.105 = (bf16[64,48,256]{2,1,0:T(8,128)(2,1)}, bf16[1024,256]{1,0:T(8,128)(2,1)}) custom-call(bf16[64,48,256]{2,1,0:T(8,128)(2,1)} %cot.3, bf16[64,32,256]{2,1,0:T(8,128)(2,1)} %copy-done.1, bf16[64,32,256]{2,1,0:T(8,128)(2,1)} %copy-done.2, bf16[64,192,384]{2,1,0:T(8,128)(2,1)} %get-tuple-element.16.matrix, bf16[1024,256]{1,0:T(8,128)(2,1)} %bitcast.34, ...), custom_call_target="tpu_custom_call" | custom-call | flops 6000000000 | bytes 20000000 | tf_op jit(solution)/shard_map/pallas_call | solution.py:227
  85.9 1.8 fusion.13
  87.7 0.6 collective-permute-start.6
  88.3 3.9 %collective-permute-start.7 = (bf16[64,32,256]{2,1,0:T(8,128)(2,1)S(1)}, bf16[64,32,256]{2,1,0:T(8,128)(2,1)}, u32[]{:S(2)}, u32[]{:S(2)}) collective-permute-start(bf16[64,32,256]{2,1,0:T(8,128)(2,1)S(1)} %get-tuple-element.24), channel_id=1, source_target_pairs={{1,0},{2,1},{3,2},{4,3},{5,4},{6,5},{7,6},{8,7},{9,8},{10,9},{11,1... | collective-permute-start | bytes 3145736 | tf_op jit(solution)/shard_map/ppermute | solution.py:161
  92.2 1.0 copy.24
  93.2 0.0 collective-permute-done.2.low
  93.2 0.0 collective-permute-done.3.high
  93.2 14.5 %shard_map.104 = (bf16[64,48,256]{2,1,0:T(8,128)(2,1)}, bf16[1024,256]{1,0:T(8,128)(2,1)}) custom-call(bf16[64,48,256]{2,1,0:T(8,128)(2,1)} %get-tuple-element.14.own, bf16[64,32,256]{2,1,0:T(8,128)(2,1)} %collective-permute-done.2.low, bf16[64,32,256]{2,1,0:T(8,128)(2,1)} %collective-permute-done.3.high, bf16[64,192,384]{2,1,0:T(8,128)(2,1)} %get-tuple-element.13.matrix, ...), custom_call_target="tpu_custom_call" | custom-call | flops 6000000000 | bytes 20000000 | tf_op jit(solution)/shard_map/pallas_call | solution.py:236
  107.7 0.0 all-reduce.4.cloned.1.call-update
  107.7 0.0 collective-permute-done.6.low
  107.7 0.0 collective-permute-done.7.high
  107.8 11.8 %shard_map.106 = bf16[64,48,256]{2,1,0:T(8,128)(2,1)} custom-call(bf16[64,48,256]{2,1,0:T(8,128)(2,1)} %get-tuple-element.19.own, bf16[64,32,256]{2,1,0:T(8,128)(2,1)} %collective-permute-done.6.low, bf16[64,32,256]{2,1,0:T(8,128)(2,1)} %collective-permute-done.7.high, bf16[64,192,384]{2,1,0:T(8,128)(2,1)} %get-tuple-element.16.matrix, ...), custom_call_target="tpu_custom_call" | custom-call | flops 6000000000 | bytes 20000000 | tf_op jit(solution)/shard_map/pallas_call | solution.py:244
  119.5 83.3 %all-reduce.4.cloned.1.call-done = (bf16[4,256,256]{2,1,0:T(8,128)(2,1)}, bf16[4,256,256]{2,1,0:T(8,128)(2,1)}) async-done(((bf16[4,256,256]{2,1,0:T(8,128)(2,1)}, bf16[4,256,256]{2,1,0:T(8,128)(2,1)}), (bf16[4,256,256]{2,1,0:T(8,128)(2,1)}, bf16[4,256,256]{2,1,0:T(8,128)(2,1)})) %all-reduce.4.cloned.1.call-update) | async-done | bytes 1048592 | tf_op jit(solution)/shard_map/psum | solution.py:235
  202.9 2.2 %reshape.100 = f32[4,256,256]{2,1,0:T(8,128)} convert(bf16[4,256,256]{2,1,0:T(8,128)(2,1)} %get-tuple-element.23) | non-fusion elementwise | flops 262144 | bytes 1572864 | tf_op jit(solution)/shard_map/reshape | solution.py:255
  205.0 1.1 reshape.98
  (16 shorter events, 0.2 us)
Async XLA Ops:
  7.2 8.7 %copy-start = (bf16[64,48,256]{2,1,0:T(8,128)(2,1)S(1)}, bf16[64,48,256]{2,1,0:T(8,128)(2,1)}, u32[]{:S(2)}) copy-start(bf16[64,48,256]{2,1,0:T(8,128)(2,1)} %cot.3) | copy-start | bytes 4718596
  7.2 195.7 %all-reduce.4.cloned.1.call-start = ((), (), s32[]{:S(2)}) async-start(), calls=%async_computation | async-start | bytes 2097152 | tf_op jit(solution)/shard_map/psum | solution.py:235
  10.4 29.3 %collective-permute-start = (bf16[64,32,256]{2,1,0:T(8,128)(2,1)}, bf16[64,32,256]{2,1,0:T(8,128)(2,1)}, u32[]{:S(2)}, u32[]{:S(2)}) collective-permute-start(bf16[64,32,256]{2,1,0:T(8,128)(2,1)} %get-tuple-element.31), channel_id=1, source_target_pairs={{0,1},{1,2},{2,3},{3,4},{4,5},{5,6},{6,7},{7,8},{8,9},{9,10},{10,1... | collective-permute-start | bytes 3145736 | tf_op jit(solution)/shard_map/ppermute | solution.py:160
  10.8 10.8 %copy-start.5 = (bf16[4,64,3,16]{1,3,2,0:T(8,128)(2,1)S(1)}, bf16[4,64,3,16]{1,3,2,0:T(8,128)(2,1)}, u32[]{:S(2)}) copy-start(bf16[4,64,3,16]{1,3,2,0:T(8,128)(2,1)} %param.8) | copy-start | bytes 73732
  10.8 11.1 %copy-start.6 = (s32[4,16]{1,0:T(4,128)S(1)}, s32[4,16]{1,0:T(4,128)}, u32[]{:S(2)}) copy-start(s32[4,16]{1,0:T(4,128)} %param.9) | copy-start | bytes 772
  10.8 11.1 %copy-start.7 = (s32[4]{0:T(128)S(1)}, s32[4]{0:T(128)}, u32[]{:S(2)}) copy-start(s32[4]{0:T(128)} %param.10) | copy-start | bytes 52
  10.8 28.8 %collective-permute-start.1 = (bf16[64,32,256]{2,1,0:T(8,128)(2,1)}, bf16[64,32,256]{2,1,0:T(8,128)(2,1)}, u32[]{:S(2)}, u32[]{:S(2)}) collective-permute-start(bf16[64,32,256]{2,1,0:T(8,128)(2,1)} %get-tuple-element.30), channel_id=1, source_target_pairs={{1,0},{2,1},{3,2},{4,3},{5,4},{6,5},{7,6},{8,7},{9,8},{10,9},{11,1... | collective-permute-start | bytes 3145736 | tf_op jit(solution)/shard_map/ppermute | solution.py:161
  17.2 49.7 %collective-permute-start.4 = (bf16[64,32,256]{2,1,0:T(8,128)(2,1)}, bf16[64,32,256]{2,1,0:T(8,128)(2,1)S(1)}, u32[]{:S(2)}, u32[]{:S(2)}) collective-permute-start(bf16[64,32,256]{2,1,0:T(8,128)(2,1)} %get-tuple-element.27), channel_id=1, source_target_pairs={{0,1},{1,2},{2,3},{3,4},{4,5},{5,6},{6,7},{7,8},{8,9},{9,10},{10,1... | collective-permute-start | bytes 3145736 | tf_op jit(solution)/shard_map/ppermute | solution.py:160
  17.2 49.7 %collective-permute-start.5 = (bf16[64,32,256]{2,1,0:T(8,128)(2,1)S(1)}, bf16[64,32,256]{2,1,0:T(8,128)(2,1)S(1)}, u32[]{:S(2)}, u32[]{:S(2)}) collective-permute-start(bf16[64,32,256]{2,1,0:T(8,128)(2,1)S(1)} %get-tuple-element.26), channel_id=1, source_target_pairs={{1,0},{2,1},{3,2},{4,3},{5,4},{6,5},{7,6},{8,7},{9,8},{10,9},{11,1... | collective-permute-start | bytes 3145736 | tf_op jit(solution)/shard_map/ppermute | solution.py:161
  56.1 37.2 %collective-permute-start.2 = (bf16[64,32,256]{2,1,0:T(8,128)(2,1)}, bf16[64,32,256]{2,1,0:T(8,128)(2,1)}, u32[]{:S(2)}, u32[]{:S(2)}) collective-permute-start(bf16[64,32,256]{2,1,0:T(8,128)(2,1)} %get-tuple-element.29), channel_id=1, source_target_pairs={{0,1},{1,2},{2,3},{3,4},{4,5},{5,6},{6,7},{7,8},{8,9},{9,10},{10,1... | collective-permute-start | bytes 3145736 | tf_op jit(solution)/shard_map/ppermute | solution.py:160
  66.8 26.4 %collective-permute-start.3 = (bf16[64,32,256]{2,1,0:T(8,128)(2,1)}, bf16[64,32,256]{2,1,0:T(8,128)(2,1)}, u32[]{:S(2)}, u32[]{:S(2)}) collective-permute-start(bf16[64,32,256]{2,1,0:T(8,128)(2,1)} %get-tuple-element.28), channel_id=1, source_target_pairs={{1,0},{2,1},{3,2},{4,3},{5,4},{6,5},{7,6},{8,7},{9,8},{10,9},{11,1... | collective-permute-start | bytes 3145736 | tf_op jit(solution)/shard_map/ppermute | solution.py:161
  66.8 1.0 copy-start.1
  66.9 1.3 copy-start.2
  85.9 6.3 %copy-start.4 = (bf16[4,256,256]{2,1,0:T(8,128)(2,1)S(1)}, bf16[4,256,256]{2,1,0:T(8,128)(2,1)}, u32[]{:S(2)}) copy-start(bf16[4,256,256]{2,1,0:T(8,128)(2,1)} %param.11) | copy-start | bytes 1572868
  87.7 20.0 %collective-permute-start.6 = (bf16[64,32,256]{2,1,0:T(8,128)(2,1)S(1)}, bf16[64,32,256]{2,1,0:T(8,128)(2,1)}, u32[]{:S(2)}, u32[]{:S(2)}) collective-permute-start(bf16[64,32,256]{2,1,0:T(8,128)(2,1)S(1)} %get-tuple-element.25), channel_id=1, source_target_pairs={{0,1},{1,2},{2,3},{3,4},{4,5},{5,6},{6,7},{7,8},{8,9},{9,10},{10,1... | collective-permute-start | bytes 3145736 | tf_op jit(solution)/shard_map/ppermute | solution.py:160
  88.3 19.4 %collective-permute-start.7 = (bf16[64,32,256]{2,1,0:T(8,128)(2,1)S(1)}, bf16[64,32,256]{2,1,0:T(8,128)(2,1)}, u32[]{:S(2)}, u32[]{:S(2)}) collective-permute-start(bf16[64,32,256]{2,1,0:T(8,128)(2,1)S(1)} %get-tuple-element.24), channel_id=1, source_target_pairs={{1,0},{2,1},{3,2},{4,3},{5,4},{6,5},{7,6},{8,7},{9,8},{10,9},{11,1... | collective-permute-start | bytes 3145736 | tf_op jit(solution)/shard_map/ppermute | solution.py:161
  202.9 2.2 %copy-start.3 = (bf16[4,256,256]{2,1,0:T(8,128)(2,1)S(1)}, bf16[4,256,256]{2,1,0:T(8,128)(2,1)}, u32[]{:S(2)}) copy-start(bf16[4,256,256]{2,1,0:T(8,128)(2,1)} %get-tuple-element.22) | copy-start | bytes 1572868
Sparse Core Ops, SparseCore 0:
  107.9 94.9 all-reduce.3
where the time goes:
time: 214 us; the launch traced here: 213 us
  waiting for transfers between devices  83.4 us (39%)
  Pallas kernels  69.9 us (33%)
  starting transfers between devices  25.3 us (12%)
  local copies, waits for them, and re-layouts  15.3 us (7%)
  between operations  14.2 us (7%)
  other arithmetic  4.44 us (2%)
    psum x1, waiting for transfers between devices, on_device(): total_first = lax.psum(grad_first, 'lon')  83.3 us
    pallas_call x1, Pallas kernels, on_device(): call(functools.partial(slope_kernel, block, scale), in_specs=common + [by...  17.7 us
    pallas_call x1, Pallas kernels, on_device(): call(functools.partial(second_kernel, block, scale), in_specs=common + [f...  14.5 us
    ppermute x4, starting transfers between devices, halos(): high = lax.ppermute(field[:, :halo], 'lon', backward)  13.4 us
    pallas_call x1, Pallas kernels, on_device(): call(functools.partial(first_kernel, block), in_specs=common, out_specs=[...  13.3 us
    pallas_call x1, Pallas kernels, on_device(): call(functools.partial(matrices_kernel, block, cols), in_specs=[table_spe...  12.5 us
    ppermute x4, starting transfers between devices, halos(): low = lax.ppermute(field[:, cols - halo:], 'lon', forward)  11.8 us
    pallas_call x1, Pallas kernels, on_device(): call(functools.partial(last_kernel, block), in_specs=common + [field_spec...  11.8 us
  transfers between devices with their start and end apart: 9, of which 1 were waited for; matrix products, arithmetic and copies ran while one was open for 6% of the time, Pallas kernels for 33%

commit v1 on v0

--- a/solution.py
+++ b/solution.py
@@ -76,6 +76,148 @@
             ]
 
 
+def greet(partners):
+    barrier = pltpu.get_barrier_semaphore()
+    for other in partners:
+        pl.semaphore_signal(
+            barrier, inc=1, device_id={"lon": other}, device_id_type=pl.DeviceIdType.MESH
+        )
+    pl.semaphore_wait(barrier, len(partners))
+
+
+def send(src, dst, send_sem, recv_sem, other):
+    return pltpu.make_async_remote_copy(
+        src_ref=src,
+        dst_ref=dst,
+        send_sem=send_sem,
+        recv_sem=recv_sem,
+        device_id={"lon": other},
+        device_id_type=pl.DeviceIdType.MESH,
+    )
+
+
+def sides(size):
+    me = lax.axis_index("lon")
+    return [lax.rem(me + 1, size), lax.rem(me + size - 1, size)]
+
+
+def edge_copies(size, field, low, high, sems):
+    right, left = sides(size)
+    cols, halo = field.shape[1], low.shape[1]
+    return [
+        send(field.at[:, pl.ds(cols - halo, halo)], low, sems.at[0], sems.at[1], right),
+        send(field.at[:, pl.ds(0, halo)], high, sems.at[2], sems.at[3], left),
+    ]
+
+
+def with_edges(size, body, spots, *refs):
+    *refs, sems = refs
+    field, low, high = (refs[spot] for spot in spots)
+    step = pl.program_id(0)
+
+    @pl.when(step == 0)
+    def _():
+        greet(sides(size))
+        for copy in edge_copies(size, field, low, high, sems):
+            copy.start()
+
+    body(*[ref for spot, ref in enumerate(refs) if spot not in spots])
+
+    @pl.when(step == pl.num_programs(0) - 1)
+    def _():
+        for copy in edge_copies(size, field, low, high, sems):
+            copy.wait()
+
+
+def partners_of(size):
+    me = lax.axis_index("lon")
+    bit0, bit1 = lax.rem(me, 2), lax.rem(me // 2, 2)
+    return [me + 1 - 2 * bit0, me + 2 - 4 * bit1] + [
+        lax.rem(me + 4 * t, size) for t in range(1, size // 4)
+    ]
+
+
+def sum_stages(size, local, buffers, total, sems):
+    got_half, half, got_quarter, quarter, got_piece, full = buffers
+    me = lax.axis_index("lon")
+    bit0, bit1, rank = lax.rem(me, 2), lax.rem(me // 2, 2), me // 4
+    group = size // 4
+    rows = local.shape[0]
+    r2, r4, rp = rows // 2, rows // 4, rows // size
+    others = partners_of(size)
+    part = lambda ref, start, count: ref.at[pl.ds(pl.multiple_of(start, 16), count)]
+    f32 = jnp.float32
+    base0 = bit0 * r2
+    base1 = base0 + bit1 * r4
+    base2 = base1 + rank * rp
+    pair = lambda i: (sems.at[2 * i], sems.at[2 * i + 1])
+
+    halves = [send(part(local, (1 - bit0) * r2, r2), got_half, *pair(0), others[0])]
+    quarters = [send(part(half, (1 - bit1) * r4, r4), got_quarter, *pair(1), others[1])]
+    pieces, spreads = [], []
+    for t in range(1, group):
+        target = lax.rem(rank + t, group)
+        pieces.append(
+            send(part(quarter, target * rp, rp), got_piece.at[t - 1], *pair(3 + t), others[1 + t])
+        )
+        mine = part(full, base2, rp)
+        spreads.append(send(mine, mine, *pair(2 + group + t), others[1 + t]))
+    mine1, mine0 = part(full, base1, r4), part(full, base0, r2)
+    back1 = [send(mine1, mine1, *pair(2), others[1])]
+    back0 = [send(mine0, mine0, *pair(3), others[0])]
+
+    def add_half():
+        half[...] = (part(local, base0, r2)[...].astype(f32) + got_half[...].astype(f32)).astype(
+            jnp.bfloat16
+        )
+
+    def add_quarter():
+        quarter[...] = (
+            part(half, bit1 * r4, r4)[...].astype(f32) + got_quarter[...].astype(f32)
+        ).astype(jnp.bfloat16)
+
+    def add_pieces():
+        acc = part(quarter, rank * rp, rp)[...].astype(f32)
+        for t in range(group - 1):
+            acc = acc + got_piece[t].astype(f32)
+        full[pl.ds(pl.multiple_of(base2, 16), rp), :] = acc.astype(jnp.bfloat16)
+
+    def finish():
+        total[...] = full[...].astype(f32)
+
+    waits = [[], halves, quarters, pieces, spreads, back1, back0]
+    works = [None, add_half, add_quarter, add_pieces, None, None, finish]
+    starts = [halves, quarters, pieces, spreads, back1, back0, []]
+
+    def stage(number):
+        def run():
+            for copy in waits[number]:
+                copy.wait()
+            if works[number] is not None:
+                works[number]()
+            for copy in starts[number]:
+                copy.start()
+
+        return run
+
+    return [stage(number) for number in range(7)]
+
+
+def sum_scratch(rows, channels, size):
+    dims = [(rows // 2,), (rows // 2,), (rows // 4,), (rows // 4,), (size // 4 - 1, rows // size), (rows,)]
+    return [pltpu.VMEM(dim + (channels,), jnp.bfloat16) for dim in dims] + [
+        pltpu.SemaphoreType.DMA((2 * (2 + 2 * (size // 4)),))
+    ]
+
+
+SUM_STEPS = (0, 1, 2, 4, 6, 7)
+
+
+def run_stages(stages, step):
+    for number, when in enumerate(SUM_STEPS):
+        pl.when(step == when)(stages[number])
+
+
 def matrices_kernel(block, cols, ahead_ref, back_ref, ahead_out, back_out):
     def body(row, carry):
         fill_matrices(ahead_ref, ahead_out, row, cols)
@@ -123,9 +265,20 @@
 
 
 def second_kernel(
-    block, scale, own, low, high, matrix, weight, resid, cot, mixed_out, grad_out, spread, grad
+    size, block, scale, own, low, high, matrix, weight, resid, cot, local, edge_field,
+    mixed_out, grad_out, total_out, edge_low, edge_high, spread, grad, *work
 ):
     step = pl.program_id(0)
+    *buffers, sum_sems, edge_sems = work
+    stages = sum_stages(size, local, buffers, total_out, sum_sems)
+
+    @pl.when(step == 0)
+    def _():
+        greet(sides(size) + partners_of(size))
+        for copy in edge_copies(size, edge_field, edge_low, edge_high, edge_sems):
+            copy.start()
+
+    run_stages(stages, step)
     spread_block(own, low, high, matrix, 0, spread, step * block, block)
     branch = jnp.dot(spread[...], weight[...], preferred_element_type=jnp.float32)
     flat = branch.shape
@@ -139,10 +292,23 @@
     @pl.when(step == pl.num_programs(0) - 1)
     def _():
         grad_out[...] = (grad[...] * scale).T.astype(jnp.bfloat16)
-
-
-def last_kernel(block, own, low, high, matrix, weight, cot, field_out, spread):
+        stages[-1]()
+        for copy in edge_copies(size, edge_field, edge_low, edge_high, edge_sems):
+            copy.wait()
+
+
+def last_kernel(
+    size, block, own, low, high, matrix, weight, cot, local, field_out, total_out, spread, *work
+):
     step = pl.program_id(0)
+    *buffers, sum_sems = work
+    stages = sum_stages(size, local, buffers, total_out, sum_sems)
+
+    @pl.when(step == 0)
+    def _():
+        greet(partners_of(size))
+
+    run_stages(stages, step)
     spread_block(own, low, high, matrix, 0, spread, step * block, block)
     adj = jnp.dot(spread[...], weight[...], preferred_element_type=jnp.float32)
     field_out[...] = (
@@ -151,15 +317,9 @@
         .reshape(field_out.shape)
     )
 
-
-def halos(field, halo):
-    count = lax.axis_size("lon")
-    cols = field.shape[1]
-    forward = [(i, (i + 1) % count) for i in range(count)]
-    backward = [(target, source) for source, target in forward]
-    low = lax.ppermute(field[:, cols - halo :], "lon", forward)
-    high = lax.ppermute(field[:, :halo], "lon", backward)
-    return low, high
+    @pl.when(step == pl.num_programs(0) - 1)
+    def _():
+        stages[-1]()
 
 
 def on_device(
@@ -178,7 +338,6 @@
     turned_second = weight_second.swapaxes(1, 2).reshape(wide, channels)
     ahead, back = tap_tables(quadrature, support, support_count, halo)
 
-    params = pltpu.CompilerParams(vmem_limit_bytes=VMEM_LIMIT)
     bf16, f32 = jnp.bfloat16, jnp.float32
     whole = lambda shape: pl.BlockSpec(shape, lambda i: (0,) * len(shape))
     by_row = lambda shape: pl.BlockSpec(shape, lambda i: (i,) + (0,) * (len(shape) - 1))
@@ -195,64 +354,85 @@
     field_type = jax.ShapeDtypeStruct((rows, cols, channels), bf16)
     grad_type = jax.ShapeDtypeStruct((wide, channels), bf16)
     work = [pltpu.VMEM(spread_shape, bf16), pltpu.VMEM((channels, wide), f32)]
-    cost = pl.CostEstimate(flops=6 * 10**9, bytes_accessed=20 * 10**6, transcendentals=0)
-
-    def call(body, **kw):
+    size = lax.axis_size("lon")
+    assert steps == 8 and size % 4 == 0
+
+    def call(number, body, **kw):
         return pl.pallas_call(
-            body, grid=(steps,), compiler_params=params, cost_estimate=cost, **kw
+            body,
+            grid=(steps,),
+            compiler_params=pltpu.CompilerParams(
+                vmem_limit_bytes=VMEM_LIMIT, collective_id=number, has_side_effects=True
+            ),
+            **kw,
         )
 
     matrix_type = jax.ShapeDtypeStruct((rows, kernels * cols, 3 * LANES), bf16)
-    act_low, act_high = halos(activations, halo)
-    cot_low, cot_high = halos(cotangent, halo)
+    halo_type = jax.ShapeDtypeStruct((rows, halo, channels), bf16)
+    total_type = jax.ShapeDtypeStruct((wide, channels), f32)
+    anywhere = pl.BlockSpec(memory_space=pl.ANY)
+    edge_sems = pltpu.SemaphoreType.DMA((4,))
     table_spec = by_row((block, kernels * 3, LANES))
-    m_ahead, m_back = call(
-        functools.partial(matrices_kernel, block, cols),
-        in_specs=[table_spec, table_spec],
-        out_specs=[matrix_spec, matrix_spec],
-        out_shape=[matrix_type, matrix_type],
-    )(ahead, back)
+    m_ahead, m_back, act_low, act_high = call(
+        0,
+        functools.partial(
+            with_edges, size, functools.partial(matrices_kernel, block, cols), (2, 5, 6)
+        ),
+        in_specs=[table_spec, table_spec, anywhere],
+        out_specs=[matrix_spec, matrix_spec, anywhere, anywhere],
+        out_shape=[matrix_type, matrix_type, halo_type, halo_type],
+        scratch_shapes=[edge_sems],
+    )(ahead, back, activations)
     cells = rows * cols
-    pre, activated, spread_one = call(
-        functools.partial(first_kernel, block),
-        in_specs=common,
-        out_specs=[by_row((block * cols, channels)), field_spec, by_row(spread_shape)],
+    pre, activated, spread_one, cot_low, cot_high = call(
+        1,
+        functools.partial(with_edges, size, functools.partial(first_kernel, block), (5, 9, 10)),
+        in_specs=common + [anywhere],
+        out_specs=[
+            by_row((block * cols, channels)), field_spec, by_row(spread_shape), anywhere, anywhere
+        ],
         out_shape=[
             jax.ShapeDtypeStruct((cells, channels), f32),
             field_type,
             jax.ShapeDtypeStruct((cells, wide), bf16),
+            halo_type,
+            halo_type,
         ],
-    )(activations, act_low, act_high, m_ahead, flat_first)
-    mid_low, mid_high = halos(activated, halo)
-    gp, grad_first = call(
-        functools.partial(slope_kernel, block, scale),
-        in_specs=common + [by_row((block * cols, channels)), by_row(spread_shape)],
+        scratch_shapes=[edge_sems],
+    )(activations, act_low, act_high, m_ahead, flat_first, cotangent)
+    gp, grad_first, mid_low, mid_high = call(
+        2,
+        functools.partial(
+            with_edges, size, functools.partial(slope_kernel, block, scale), (7, 10, 11)
+        ),
+        in_specs=common + [by_row((block * cols, channels)), by_row(spread_shape), anywhere],
+        out_specs=[field_spec, whole((wide, channels)), anywhere, anywhere],
+        out_shape=[field_type, grad_type, halo_type, halo_type],
+        scratch_shapes=work + [edge_sems],
+    )(cotangent, cot_low, cot_high, m_back, turned_second, pre, spread_one, activated)
+    mixed, grad_second, total_first, gp_low, gp_high = call(
+        3,
+        functools.partial(second_kernel, size, block, scale),
+        in_specs=common + [field_spec, field_spec, whole((wide, channels)), anywhere],
+        out_specs=[
+            field_spec, whole((wide, channels)), whole((wide, channels)), anywhere, anywhere
+        ],
+        out_shape=[field_type, grad_type, total_type, halo_type, halo_type],
+        scratch_shapes=work + sum_scratch(wide, channels, size) + [edge_sems],
+    )(activated, mid_low, mid_high, m_ahead, flat_second, activations, cotangent, grad_first, gp)
+    grad_field, total_second = call(
+        4,
+        functools.partial(last_kernel, size, block),
+        in_specs=common + [field_spec, whole((wide, channels))],
         out_specs=[field_spec, whole((wide, channels))],
-        out_shape=[field_type, grad_type],
-        scratch_shapes=work,
-    )(cotangent, cot_low, cot_high, m_back, turned_second, pre, spread_one)
-    gp_low, gp_high = halos(gp, halo)
-    total_first = lax.psum(grad_first, "lon")
-    mixed, grad_second = call(
-        functools.partial(second_kernel, block, scale),
-        in_specs=common + [field_spec, field_spec],
-        out_specs=[field_spec, whole((wide, channels))],
-        out_shape=[field_type, grad_type],
-        scratch_shapes=work,
-    )(activated, mid_low, mid_high, m_ahead, flat_second, activations, cotangent)
-    total_second = lax.psum(grad_second, "lon")
-    grad_field = call(
-        functools.partial(last_kernel, block),
-        in_specs=common + [field_spec],
-        out_specs=field_spec,
-        out_shape=field_type,
-        scratch_shapes=work[:1],
-    )(gp, gp_low, gp_high, m_back, turned_first, cotangent)
+        out_shape=[field_type, total_type],
+        scratch_shapes=work[:1] + sum_scratch(wide, channels, size),
+    )(gp, gp_low, gp_high, m_back, turned_first, cotangent, grad_second)
     return (
         mixed,
         grad_field,
-        total_first.astype(f32).reshape(kernels, channels, channels),
-        total_second.astype(f32).reshape(kernels, channels, channels),
+        total_first.reshape(kernels, channels, channels),
+        total_second.reshape(kernels, channels, channels),
     )
 
 

time: 214 us -> 180 us (0.84)
  Pallas kernels: 69.9 us -> 164 us
  waiting for transfers between devices: 83.4 us -> 0 us
  starting transfers between devices: 25.3 us -> 0 us
  between operations: 14.2 us -> 0.8 us
  local copies, waits for them, and re-layouts: 15.3 us -> 10.7 us
    pallas_call x5, Pallas kernels: 69.9 us -> 164 us  [the longest x1 58.3 us: on_device(): call(3, functools.partial(second_kernel, size, block, scale), in_specs=co...]
    psum x1 -> x0, waiting for transfers between devices: 83.3 us -> none  [on_device(): total_first = lax.psum(grad_first, 'lon')]
    ppermute x8 -> x0, starting transfers between devices: 25.2 us -> none  [the longest x4 13.4 us: halos(): high = lax.ppermute(field[:, :halo], 'lon', backward)]
    slice x4 -> x0, local copies, waits for them, and re-layouts: 9.27 us -> none  [halos(): high = lax.ppermute(field[:, :halo], 'lon', backward)]
    unnamed x16, local copies, waits for them, and re-layouts: 1.36 us -> 6.35 us
    reshape x2 -> x0, other arithmetic: 3.22 us -> none  [the longest x1 2.16 us: on_device(): total_second.astype(f32).reshape(kernels, channels, channels)]
  transfers between devices with their start and end apart: 9 -> 0, of which waited for: 1 -> 0; matrix products, arithmetic and copies ran while one was open for 6% -> 0% of each run, Pallas kernels for 33% -> 0%
where the time goes in v1:
time: 180 us; the launch traced here: 179 us
  Pallas kernels  164 us (91%)
  local copies, waits for them, and re-layouts  10.7 us (6%)
  other arithmetic  2.56 us (1%)
    pallas_call x1, Pallas kernels, on_device(): call(3, functools.partial(second_kernel, size, block, scale), in_specs=co...  58.3 us
    pallas_call x1, Pallas kernels, on_device(): call(1, functools.partial(with_edges, size, functools.partial(first_kerne...  29.5 us
    pallas_call x1, Pallas kernels, on_device(): call(2, functools.partial(with_edges, size, functools.partial(slope_kerne...  28.3 us
    pallas_call x1, Pallas kernels, on_device(): call(4, functools.partial(last_kernel, size, block), in_specs=common + [f...  26.5 us
    pallas_call x1, Pallas kernels, on_device(): call(0, functools.partial(with_edges, size, functools.partial(matrices_ke...  21.4 us
    unnamed x16, local copies, waits for them, and re-layouts  6.35 us

profile of v1, /device:TPU:0, one launch (start us, length us, event | category | flops | bytes accessed | tf_op | source)
XLA Modules:
  0.0 178.7 jit_solution(7775493821623791922)
XLA Ops:
  0.6 0.9 reshape.83
  1.6 0.2 copy.17
  1.8 0.7 multiply_add_fusion
  2.4 0.7 iota_compare_fusion.2
  3.2 0.3 convolution_bitcast_fusion
  3.6 1.0 copy.22.refs_1_
  4.6 0.3 convolution_bitcast_fusion.1
  4.9 0.1 copy.16
  5.0 1.1 copy_select_fusion.refs_0_
  6.2 21.4 %shard_map.102 = (bf16[64,192,384]{2,1,0:T(8,128)(2,1)}, bf16[64,192,384]{2,1,0:T(8,128)(2,1)}, bf16[64,32,256]{2,1,0:T(8,128)(2,1)}, bf16[64,32,256]{2,1,0:T(8,128)(2,1)}) custom-call(f32[64,12,128]{2,1,0:T(8,128)} %copy_select_fusion.refs_0_, f32[64,12,128]{2,1,0:T(8,128)} %copy.22.refs_1_, bf16[64,48,256]{2,1,0:T(8,128)(2,1)} %resid.1), custom_call_target="tpu_custom_call" | custom-call | tf_op jit(solution)/shard_map/pallas_call | solution.py:376
  27.6 0.0 copy-start
  27.6 29.5 %shard_map.103 = (f32[3072,256]{1,0:T(8,128)}, bf16[64,48,256]{2,1,0:T(8,128)(2,1)}, bf16[3072,1024]{1,0:T(8,128)(2,1)}, bf16[64,32,256]{2,1,0:T(8,128)(2,1)}, bf16[64,32,256]{2,1,0:T(8,128)(2,1)}) custom-call(bf16[64,48,256]{2,1,0:T(8,128)(2,1)} %resid.1, bf16[64,32,256]{2,1,0:T(8,128)(2,1)} %get-tuple-element.24.refs_1_, ...), custom_call_target="tpu_custom_call" | custom-call | tf_op jit(solution)/shard_map/pallas_call | solution.py:387
  57.1 0.0 copy-done
  57.1 1.0 copy.23
  58.1 28.3 %shard_map.104 = (bf16[64,48,256]{2,1,0:T(8,128)(2,1)}, bf16[1024,256]{1,0:T(8,128)(2,1)}, bf16[64,32,256]{2,1,0:T(8,128)(2,1)}, bf16[64,32,256]{2,1,0:T(8,128)(2,1)}) custom-call(bf16[64,48,256]{2,1,0:T(8,128)(2,1)} %cot.3, bf16[64,32,256]{2,1,0:T(8,128)(2,1)} %get-tuple-element.28.refs_1_, bf16[64,32,256]{2,1,0:T(8,128)(2,1)} %get-tuple-element.29.refs_2_, ...), custom_call_target="tpu_custom_call" | custom-call | tf_op jit(solution)/shard_map/pallas_call | solution.py:403
  86.4 0.0 copy-start.1
  86.4 58.3 %shard_map.105 = (bf16[64,48,256]{2,1,0:T(8,128)(2,1)}, bf16[1024,256]{1,0:T(8,128)(2,1)}, f32[1024,256]{1,0:T(8,128)}, bf16[64,32,256]{2,1,0:T(8,128)(2,1)}, bf16[64,32,256]{2,1,0:T(8,128)(2,1)}) custom-call(bf16[64,48,256]{2,1,0:T(8,128)(2,1)} %get-tuple-element.27.refs_7_.own, bf16[64,32,256]{2,1,0:T(8,128)(2,1)} %get-tuple-element.33.low, ...), custom_call_target="tpu_custom_call" | custom-call | tf_op jit(solution)/shard_map/pallas_call | solution.py:413
  144.7 0.0 copy-done.1
  144.7 1.0 copy.24
  145.7 0.0 copy-start.2
  145.7 26.5 %shard_map.106 = (bf16[64,48,256]{2,1,0:T(8,128)(2,1)}, f32[1024,256]{1,0:T(8,128)}) custom-call(bf16[64,48,256]{2,1,0:T(8,128)(2,1)} %get-tuple-element.36.edge_field.own, bf16[64,32,256]{2,1,0:T(8,128)(2,1)} %get-tuple-element.38.low, bf16[64,32,256]{2,1,0:T(8,128)(2,1)} %get-tuple-element.39.high, bf16[64,192,384]{2,1,0:T(8,128)(2,1)} %get-tuple-element.30.refs_3_.matrix, ...), custom_call_target="tpu_custom_call" | custom-call | tf_op jit(solution)/shard_map/pallas_call | solution.py:423
  172.3 0.0 copy-done.2
  172.3 0.0 copy-start.3
  172.3 1.1 copy.32
  173.5 0.8 copy-done.3
  174.3 0.0 copy-start.4
  174.3 1.1 copy.33
  175.4 0.6 copy-done.4
  176.1 0.0 copy-start.5
  176.1 1.0 copy.34
  177.0 0.6 copy-done.5
  177.7 1.0 copy.35
  (7 shorter events, 0.2 us)
Async XLA Ops:
  27.6 29.5 %copy-start = (bf16[4,256,256]{2,1,0:T(8,128)(2,1)S(1)}, bf16[4,256,256]{2,1,0:T(8,128)(2,1)}, u32[]{:S(2)}) copy-start(bf16[4,256,256]{2,1,0:T(8,128)(2,1)} %param.12) | copy-start | bytes 1572868
  86.4 58.3 %copy-start.1 = (bf16[4,256,256]{2,1,0:T(8,128)(2,1)S(1)}, bf16[4,256,256]{2,1,0:T(8,128)(2,1)}, u32[]{:S(2)}) copy-start(bf16[4,256,256]{2,1,0:T(8,128)(2,1)} %param.11) | copy-start | bytes 1572868
  145.7 26.6 %copy-start.2 = (bf16[64,48,256]{2,1,0:T(8,128)(2,1)S(1)}, bf16[64,48,256]{2,1,0:T(8,128)(2,1)}, u32[]{:S(2)}) copy-start(bf16[64,48,256]{2,1,0:T(8,128)(2,1)} %get-tuple-element.53) | copy-start | bytes 4718596
  172.3 2.0 %copy-start.3 = (bf16[64,48,256]{2,1,0:T(8,128)(2,1)S(1)}, bf16[64,48,256]{2,1,0:T(8,128)(2,1)}, u32[]{:S(2)}) copy-start(bf16[64,48,256]{2,1,0:T(8,128)(2,1)} %get-tuple-element.54) | copy-start | bytes 4718596
  174.3 1.8 %copy-start.4 = (f32[1024,256]{1,0:T(8,128)S(1)}, f32[1024,256]{1,0:T(8,128)}, u32[]{:S(2)}) copy-start(f32[1024,256]{1,0:T(8,128)} %get-tuple-element.42) | copy-start | bytes 3145732
  176.1 1.6 copy-start.5

commit v2 on v1

--- a/solution.py
+++ b/solution.py
@@ -101,31 +101,67 @@
     return [lax.rem(me + 1, size), lax.rem(me + size - 1, size)]
 
 
-def edge_copies(size, field, low, high, sems):
+NARROW = 16
+
+
+def pack_edges(field, to_right, to_left):
+    cols = field.shape[1]
+    pairs, width = to_right.shape[0], to_right.shape[1] // 2
+    first = field.shape[0] - 2 * pairs
+    for p in range(pairs):
+        two = [field[first + 2 * p], field[first + 2 * p + 1]]
+        to_right[p] = jnp.concatenate([row[cols - width :] for row in two], 0)
+        to_left[p] = jnp.concatenate([row[:width] for row in two], 0)
+
+
+def unpack_edges(edges, low, high):
+    near_low, near_high, far_low, far_high = edges
+    near, halo, channels = near_low.shape[0], low.shape[1], low.shape[2]
+    pairs, width = far_low.shape[0], far_low.shape[1] // 2
+    blank = jnp.zeros((near, halo - NARROW, channels), low.dtype)
+    low[:near, : halo - NARROW] = blank
+    low[:near, halo - NARROW :] = near_low[...]
+    high[:near, :NARROW] = near_high[...]
+    high[:near, NARROW:] = blank
+    blank = jnp.zeros((halo - width, channels), low.dtype)
+    for p in range(pairs):
+        below, above = far_low[p], far_high[p]
+        for q in range(2):
+            cut = slice(q * width, (q + 1) * width)
+            low[near + 2 * p + q] = jnp.concatenate([blank, below[cut]], 0)
+            high[near + 2 * p + q] = jnp.concatenate([above[cut], blank], 0)
+
+
+def edge_copies(size, field, to_right, to_left, edges, sems):
     right, left = sides(size)
-    cols, halo = field.shape[1], low.shape[1]
+    near_low, near_high, far_low, far_high = edges
+    cols, near = field.shape[1], near_low.shape[0]
+    rows = pl.ds(0, near)
     return [
-        send(field.at[:, pl.ds(cols - halo, halo)], low, sems.at[0], sems.at[1], right),
-        send(field.at[:, pl.ds(0, halo)], high, sems.at[2], sems.at[3], left),
+        send(field.at[rows, pl.ds(cols - NARROW, NARROW)], near_low, sems.at[0], sems.at[1], right),
+        send(field.at[rows, pl.ds(0, NARROW)], near_high, sems.at[2], sems.at[3], left),
+        send(to_right, far_low, sems.at[4], sems.at[5], right),
+        send(to_left, far_high, sems.at[6], sems.at[7], left),
     ]
 
 
-def with_edges(size, body, spots, *refs):
-    *refs, sems = refs
-    field, low, high = (refs[spot] for spot in spots)
+def with_edges(size, body, at_field, at_edges, *refs):
+    *refs, to_right, to_left, sems = refs
+    field, edges = refs[at_field], refs[at_edges : at_edges + 4]
     step = pl.program_id(0)
 
     @pl.when(step == 0)
     def _():
+        pack_edges(field, to_right, to_left)
         greet(sides(size))
-        for copy in edge_copies(size, field, low, high, sems):
+        for copy in edge_copies(size, field, to_right, to_left, edges, sems):
             copy.start()
 
-    body(*[ref for spot, ref in enumerate(refs) if spot not in spots])
+    body(*refs[:at_field], *refs[at_field + 1 : at_edges], *refs[at_edges + 4 :])
 
     @pl.when(step == pl.num_programs(0) - 1)
     def _():
-        for copy in edge_copies(size, field, low, high, sems):
+        for copy in edge_copies(size, field, to_right, to_left, edges, sems):
             copy.wait()
 
 
@@ -183,7 +219,8 @@
         full[pl.ds(pl.multiple_of(base2, 16), rp), :] = acc.astype(jnp.bfloat16)
 
     def finish():
-        total[...] = full[...].astype(f32)
+        total[0][...] = full[: rows // 2].astype(f32)
+        total[1][...] = full[rows // 2 :].astype(f32)
 
     waits = [[], halves, quarters, pieces, spreads, back1, back0]
     works = [None, add_half, add_quarter, add_pieces, None, None, finish]
@@ -210,11 +247,11 @@
     ]
 
 
-SUM_STEPS = (0, 1, 2, 4, 6, 7)
+SUM_STEPS = (1, 3, 5, 6, 7)
 
 
 def run_stages(stages, step):
-    for number, when in enumerate(SUM_STEPS):
+    for number, when in enumerate(SUM_STEPS, 1):
         pl.when(step == when)(stages[number])
 
 
@@ -241,8 +278,9 @@
         grad_ref[...] += part
 
 
-def first_kernel(block, own, low, high, matrix, weight, pre_out, act_out, spread_out):
+def first_kernel(block, own, e0, e1, e2, e3, matrix, weight, pre_out, act_out, spread_out, low, high):
     step = pl.program_id(0)
+    pl.when(step == 0)(lambda: unpack_edges((e0, e1, e2, e3), low, high))
     spread_block(own, low, high, matrix, 0, spread_out, step * block, block)
     pre = jnp.dot(spread_out[...], weight[...], preferred_element_type=jnp.float32)
     pre_out[...] = pre
@@ -250,9 +288,11 @@
 
 
 def slope_kernel(
-    block, scale, own, low, high, matrix, weight, pre, spread_one, gp_out, grad_out, spread, grad
+    block, scale, own, e0, e1, e2, e3, matrix, weight, pre, spread_one, gp_out, grad_out,
+    low, high, spread, grad,
 ):
     step = pl.program_id(0)
+    pl.when(step == 0)(lambda: unpack_edges((e0, e1, e2, e3), low, high))
     spread_block(own, low, high, matrix, 0, spread, step * block, block)
     grad_act = jnp.dot(spread[...], weight[...], preferred_element_type=jnp.float32)
     gp = (grad_act * gelu_slope(pre[...])).astype(jnp.bfloat16)
@@ -265,20 +305,11 @@
 
 
 def second_kernel(
-    size, block, scale, own, low, high, matrix, weight, resid, cot, local, edge_field,
-    mixed_out, grad_out, total_out, edge_low, edge_high, spread, grad, *work
+    block, scale, own, e0, e1, e2, e3, matrix, weight, resid, cot, mixed_out, grad_out,
+    low, high, spread, grad,
 ):
     step = pl.program_id(0)
-    *buffers, sum_sems, edge_sems = work
-    stages = sum_stages(size, local, buffers, total_out, sum_sems)
-
-    @pl.when(step == 0)
-    def _():
-        greet(sides(size) + partners_of(size))
-        for copy in edge_copies(size, edge_field, edge_low, edge_high, edge_sems):
-            copy.start()
-
-    run_stages(stages, step)
+    pl.when(step == 0)(lambda: unpack_edges((e0, e1, e2, e3), low, high))
     spread_block(own, low, high, matrix, 0, spread, step * block, block)
     branch = jnp.dot(spread[...], weight[...], preferred_element_type=jnp.float32)
     flat = branch.shape
@@ -292,21 +323,24 @@
     @pl.when(step == pl.num_programs(0) - 1)
     def _():
         grad_out[...] = (grad[...] * scale).T.astype(jnp.bfloat16)
-        stages[-1]()
-        for copy in edge_copies(size, edge_field, edge_low, edge_high, edge_sems):
-            copy.wait()
 
 
 def last_kernel(
-    size, block, own, low, high, matrix, weight, cot, local, field_out, total_out, spread, *work
+    size, block, own, e0, e1, e2, e3, matrix, weight, cot, grad_first, grad_second,
+    field_out, total_first, total_second, low, high, spread, local, *work
 ):
     step = pl.program_id(0)
     *buffers, sum_sems = work
-    stages = sum_stages(size, local, buffers, total_out, sum_sems)
+    wide = grad_first.shape[0]
+    stages = sum_stages(size, local, buffers, (total_first, total_second), sum_sems)
 
     @pl.when(step == 0)
     def _():
+        local[:wide] = grad_first[...]
+        local[wide:] = grad_second[...]
         greet(partners_of(size))
+        stages[0]()
+        unpack_edges((e0, e1, e2, e3), low, high)
 
     run_stages(stages, step)
     spread_block(own, low, high, matrix, 0, spread, step * block, block)
@@ -343,13 +377,17 @@
     by_row = lambda shape: pl.BlockSpec(shape, lambda i: (i,) + (0,) * (len(shape) - 1))
     field_spec = by_row((block, cols, channels))
     matrix_spec = by_row((block, kernels * cols, 3 * LANES))
-    common = [
-        whole((rows, cols, channels)),
-        whole((rows, halo, channels)),
-        whole((rows, halo, channels)),
-        matrix_spec,
-        whole((wide, channels)),
-    ]
+    bands = support.shape[0]
+    wider = [b for b in range(bands) if (cols // 2) * (b + 1) // bands > NARROW]
+    near = max((min(wider) * (rows // bands) - 1) // 2 * 2, 2)
+    near_shape = (near, NARROW, channels)
+    far_shape = ((rows - near) // 2, 2 * (cols // 2), channels)
+    edge_shapes = [near_shape, near_shape, far_shape, far_shape]
+    common = (
+        [whole((rows, cols, channels))]
+        + [whole(shape) for shape in edge_shapes]
+        + [matrix_spec, whole((wide, channels))]
+    )
     spread_shape = (block * cols, wide)
     field_type = jax.ShapeDtypeStruct((rows, cols, channels), bf16)
     grad_type = jax.ShapeDtypeStruct((wide, channels), bf16)
@@ -368,66 +406,67 @@
         )
 
     matrix_type = jax.ShapeDtypeStruct((rows, kernels * cols, 3 * LANES), bf16)
-    halo_type = jax.ShapeDtypeStruct((rows, halo, channels), bf16)
+    edge_types = [jax.ShapeDtypeStruct(shape, bf16) for shape in edge_shapes]
+    field_whole = whole((rows, cols, channels))
+    unpacked = [pltpu.VMEM((rows, halo, channels), bf16)] * 2
     total_type = jax.ShapeDtypeStruct((wide, channels), f32)
     anywhere = pl.BlockSpec(memory_space=pl.ANY)
-    edge_sems = pltpu.SemaphoreType.DMA((4,))
+    edge_work = [pltpu.VMEM(far_shape, bf16)] * 2 + [pltpu.SemaphoreType.DMA((8,))]
     table_spec = by_row((block, kernels * 3, LANES))
-    m_ahead, m_back, act_low, act_high = call(
+    edged = lambda body, at_field, at_edges: functools.partial(
+        with_edges, size, body, at_field, at_edges
+    )
+    m_ahead, m_back, *act_edges = call(
         0,
-        functools.partial(
-            with_edges, size, functools.partial(matrices_kernel, block, cols), (2, 5, 6)
-        ),
-        in_specs=[table_spec, table_spec, anywhere],
-        out_specs=[matrix_spec, matrix_spec, anywhere, anywhere],
-        out_shape=[matrix_type, matrix_type, halo_type, halo_type],
-        scratch_shapes=[edge_sems],
+        edged(functools.partial(matrices_kernel, block, cols), 2, 5),
+        in_specs=[table_spec, table_spec, field_whole],
+        out_specs=[matrix_spec, matrix_spec] + [anywhere] * 4,
+        out_shape=[matrix_type, matrix_type] + edge_types,
+        scratch_shapes=edge_work,
     )(ahead, back, activations)
     cells = rows * cols
-    pre, activated, spread_one, cot_low, cot_high = call(
+    pre, activated, spread_one, *cot_edges = call(
         1,
-        functools.partial(with_edges, size, functools.partial(first_kernel, block), (5, 9, 10)),
-        in_specs=common + [anywhere],
-        out_specs=[
-            by_row((block * cols, channels)), field_spec, by_row(spread_shape), anywhere, anywhere
-        ],
+        edged(functools.partial(first_kernel, block), 7, 11),
+        in_specs=common + [field_whole],
+        out_specs=[by_row((block * cols, channels)), field_spec, by_row(spread_shape)]
+        + [anywhere] * 4,
         out_shape=[
             jax.ShapeDtypeStruct((cells, channels), f32),
             field_type,
             jax.ShapeDtypeStruct((cells, wide), bf16),
-            halo_type,
-            halo_type,
-        ],
-        scratch_shapes=[edge_sems],
-    )(activations, act_low, act_high, m_ahead, flat_first, cotangent)
-    gp, grad_first, mid_low, mid_high = call(
+        ]
+        + edge_types,
+        scratch_shapes=unpacked + edge_work,
+    )(activations, *act_edges, m_ahead, flat_first, cotangent)
+    gp, grad_first, *mid_edges = call(
         2,
-        functools.partial(
-            with_edges, size, functools.partial(slope_kernel, block, scale), (7, 10, 11)
-        ),
-        in_specs=common + [by_row((block * cols, channels)), by_row(spread_shape), anywhere],
-        out_specs=[field_spec, whole((wide, channels)), anywhere, anywhere],
-        out_shape=[field_type, grad_type, halo_type, halo_type],
-        scratch_shapes=work + [edge_sems],
-    )(cotangent, cot_low, cot_high, m_back, turned_second, pre, spread_one, activated)
-    mixed, grad_second, total_first, gp_low, gp_high = call(
+        edged(functools.partial(slope_kernel, block, scale), 9, 12),
+        in_specs=common + [by_row((block * cols, channels)), by_row(spread_shape), field_whole],
+        out_specs=[field_spec, whole((wide, channels))] + [anywhere] * 4,
+        out_shape=[field_type, grad_type] + edge_types,
+        scratch_shapes=unpacked + work + edge_work,
+    )(cotangent, *cot_edges, m_back, turned_second, pre, spread_one, activated)
+    mixed, grad_second, *gp_edges = call(
         3,
-        functools.partial(second_kernel, size, block, scale),
-        in_specs=common + [field_spec, field_spec, whole((wide, channels)), anywhere],
-        out_specs=[
-            field_spec, whole((wide, channels)), whole((wide, channels)), anywhere, anywhere
-        ],
-        out_shape=[field_type, grad_type, total_type, halo_type, halo_type],
-        scratch_shapes=work + sum_scratch(wide, channels, size) + [edge_sems],
-    )(activated, mid_low, mid_high, m_ahead, flat_second, activations, cotangent, grad_first, gp)
-    grad_field, total_second = call(
+        edged(functools.partial(second_kernel, block, scale), 9, 12),
+        in_specs=common + [field_spec, field_spec, field_whole],
+        out_specs=[field_spec, whole((wide, channels))] + [anywhere] * 4,
+        out_shape=[field_type, grad_type] + edge_types,
+        scratch_shapes=unpacked + work + edge_work,
+    )(activated, *mid_edges, m_ahead, flat_second, activations, cotangent, gp)
+    grad_spec = whole((wide, channels))
+    grad_field, total_first, total_second = call(
         4,
         functools.partial(last_kernel, size, block),
-        in_specs=common + [field_spec, whole((wide, channels))],
-        out_specs=[field_spec, whole((wide, channels))],
-        out_shape=[field_type, total_type],
-        scratch_shapes=work[:1] + sum_scratch(wide, channels, size),
-    )(gp, gp_low, gp_high, m_back, turned_first, cotangent, grad_second)
+        in_specs=common + [field_spec, grad_spec, grad_spec],
+        out_specs=[field_spec, grad_spec, grad_spec],
+        out_shape=[field_type, total_type, total_type],
+        scratch_shapes=unpacked
+        + work[:1]
+        + [pltpu.VMEM((2 * wide, channels), bf16)]
+        + sum_scratch(2 * wide, channels, size),
+    )(gp, *gp_edges, m_back, turned_first, cotangent, grad_first, grad_second)
     return (
         mixed,
         grad_field,

time: 180 us -> 140 us (0.78)
  Pallas kernels: 164 us -> 124 us
    pallas_call x4, Pallas kernels: 138 us -> 80.9 us  [the longest x1 22.4 us: on_device(): call(2, edged(functools.partial(slope_kernel, block, scale), 9, 12), in_s...]
    pallas_call x1, Pallas kernels: 26.5 us -> 43.3 us  [on_device(): call(4, functools.partial(last_kernel, size, block), in_specs=common + [f...]
where the time goes in v2:
time: 140 us; the launch traced here: 139 us
  Pallas kernels  124 us (89%)
  local copies, waits for them, and re-layouts  10.7 us (8%)
  other arithmetic  2.56 us (2%)
    pallas_call x1, Pallas kernels, on_device(): call(4, functools.partial(last_kernel, size, block), in_specs=common + [f...  43.3 us
    pallas_call x1, Pallas kernels, on_device(): call(2, edged(functools.partial(slope_kernel, block, scale), 9, 12), in_s...  22.4 us
    pallas_call x1, Pallas kernels, on_device(): call(1, edged(functools.partial(first_kernel, block), 7, 11), in_specs=co...  20.5 us
    pallas_call x1, Pallas kernels, on_device(): call(3, edged(functools.partial(second_kernel, block, scale), 9, 12), in_...  19.3 us
    pallas_call x1, Pallas kernels, on_device(): call(0, edged(functools.partial(matrices_kernel, block, cols), 2, 5), in_...  18.8 us
    unnamed x16, local copies, waits for them, and re-layouts  6.35 us

profile of v2, /device:TPU:0, one launch (start us, length us, event | category | flops | bytes accessed | tf_op | source)
XLA Modules:
  0.0 138.8 jit_solution(14843090035825979683)
XLA Ops:
  0.6 0.9 reshape.83
  1.6 0.2 copy.17
  1.8 0.7 multiply_add_fusion
  2.4 0.7 iota_compare_fusion.2
  3.2 0.3 convolution_bitcast_fusion
  3.6 1.0 copy.22.refs_1_
  4.6 0.3 convolution_bitcast_fusion.1
  4.9 0.1 copy.16
  5.0 1.1 copy_select_fusion.refs_0_
  6.2 18.8 %shard_map.102 = (bf16[64,192,384]{2,1,0:T(8,128)(2,1)}, bf16[64,192,384]{2,1,0:T(8,128)(2,1)}, bf16[30,16,256]{2,1,0:T(8,128)(2,1)}, bf16[30,16,256]{2,1,0:T(8,...) custom-call(f32[64,12,128]{2,1,0:T(8,128)} %copy_select_fusion.refs_0_, ...), custom_call_target="tpu_custom_call" | custom-call | tf_op jit(solution)/shard_map/pallas_call | solution.py:419
  24.9 0.0 copy-start
  24.9 20.5 %shard_map.103 = (f32[3072,256]{1,0:T(8,128)}, bf16[64,48,256]{2,1,0:T(8,128)(2,1)}, bf16[3072,1024]{1,0:T(8,128)(2,1)}, bf16[30,16,256]{2,1,0:T(8,128)(2,1)}, b...) custom-call(bf16[64,48,256]{2,1,0:T(8,128)(2,1)} %refs_7_.3, ...), custom_call_target="tpu_custom_call" | custom-call | tf_op jit(solution)/shard_map/pallas_call | solution.py:428
  45.4 0.0 copy-done
  45.4 1.0 copy.23
  46.4 22.4 %shard_map.104 = (bf16[64,48,256]{2,1,0:T(8,128)(2,1)}, bf16[1024,256]{1,0:T(8,128)(2,1)}, bf16[30,16,256]{2,1,0:T(8,128)(2,1)}, bf16[30,16,256]{2,1,0:T(8,128)(...) custom-call(bf16[64,48,256]{2,1,0:T(8,128)(2,1)} %cot.1, ...), custom_call_target="tpu_custom_call" | custom-call | tf_op jit(solution)/shard_map/pallas_call | solution.py:442
  68.8 0.0 copy-start.1
  68.8 19.3 %shard_map.105 = (bf16[64,48,256]{2,1,0:T(8,128)(2,1)}, bf16[1024,256]{1,0:T(8,128)(2,1)}, bf16[30,16,256]{2,1,0:T(8,128)(2,1)}, bf16[30,16,256]{2,1,0:T(8,128)(...) custom-call(bf16[64,48,256]{2,1,0:T(8,128)(2,1)} %get-tuple-element.37.refs_9_.refs_0_, ...), custom_call_target="tpu_custom_call" | custom-call | tf_op jit(solution)/shard_map/pallas_call | solution.py:450
  88.1 0.0 copy-done.1
  88.1 1.0 copy.24
  89.1 0.0 copy-start.2
  89.1 43.3 %shard_map.106 = (bf16[64,48,256]{2,1,0:T(8,128)(2,1)}, f32[1024,256]{1,0:T(8,128)}, f32[1024,256]{1,0:T(8,128)}) custom-call(bf16[64,48,256]{2,1,0:T(8,128)(2,1)} %get-tuple-element.49.refs_9_.own, bf16[30,16,256]{2,1,0:T(8,128)(2,1)} %get-tuple-element.51.e0, bf16[30,16,256]{2,1,0:T(8,128)(2,1)} %get-tuple-element.52.e1, ...), custom_call_target="tpu_custom_call" | custom-call | tf_op jit(solution)/shard_map/pallas_call | solution.py:459
  132.4 0.0 copy-done.2
  132.4 0.0 copy-start.3
  132.5 1.1 copy.32
  133.6 0.8 copy-done.3
  134.4 0.0 copy-start.5
  134.4 1.1 copy.33
  135.6 0.6 copy-done.5
  136.2 0.0 copy-start.4
  136.2 1.0 copy.34
  137.2 0.6 copy-done.4
  137.8 1.0 copy.35
  (7 shorter events, 0.2 us)
Async XLA Ops:
  24.9 20.5 %copy-start = (bf16[4,256,256]{2,1,0:T(8,128)(2,1)S(1)}, bf16[4,256,256]{2,1,0:T(8,128)(2,1)}, u32[]{:S(2)}) copy-start(bf16[4,256,256]{2,1,0:T(8,128)(2,1)} %param.12) | copy-start | bytes 1572868
  68.8 19.3 %copy-start.1 = (bf16[4,256,256]{2,1,0:T(8,128)(2,1)S(1)}, bf16[4,256,256]{2,1,0:T(8,128)(2,1)}, u32[]{:S(2)}) copy-start(bf16[4,256,256]{2,1,0:T(8,128)(2,1)} %param.11) | copy-start | bytes 1572868
  89.1 43.3 %copy-start.2 = (bf16[64,48,256]{2,1,0:T(8,128)(2,1)S(1)}, bf16[64,48,256]{2,1,0:T(8,128)(2,1)}, u32[]{:S(2)}) copy-start(bf16[64,48,256]{2,1,0:T(8,128)(2,1)} %get-tuple-element.69) | copy-start | bytes 4718596
  132.4 2.0 %copy-start.3 = (bf16[64,48,256]{2,1,0:T(8,128)(2,1)S(1)}, bf16[64,48,256]{2,1,0:T(8,128)(2,1)}, u32[]{:S(2)}) copy-start(bf16[64,48,256]{2,1,0:T(8,128)(2,1)} %get-tuple-element.70) | copy-start | bytes 4718596
  134.4 1.8 %copy-start.5 = (f32[1024,256]{1,0:T(8,128)S(1)}, f32[1024,256]{1,0:T(8,128)}, u32[]{:S(2)}) copy-start(f32[1024,256]{1,0:T(8,128)} %get-tuple-element.58) | copy-start | bytes 3145732
  136.2 1.6 %copy-start.4 = (f32[1024,256]{1,0:T(8,128)S(1)}, f32[1024,256]{1,0:T(8,128)}, u32[]{:S(2)}) copy-start(f32[1024,256]{1,0:T(8,128)} %get-tuple-element.59) | copy-start | bytes 3145732

commit v3 on v2

--- a/solution.py
+++ b/solution.py
@@ -9,6 +9,7 @@
 from jax.sharding import PartitionSpec as P
 
 LANES = 128
+GRAIN = 4
 VMEM_LIMIT = 56 * 1024 * 1024
 
 
@@ -101,67 +102,68 @@
     return [lax.rem(me + 1, size), lax.rem(me + size - 1, size)]
 
 
-NARROW = 16
-
-
-def pack_edges(field, to_right, to_left):
+def edge_widths(rows, bands, widest):
+    reach = [widest * (i // (rows // bands) + 1) // bands for i in range(rows)]
+    return [-(-max(reach[max(i - 1, 0) : i + 2]) // GRAIN) * GRAIN for i in range(rows)]
+
+
+def pack_edges(widths, field, to_right, to_left):
     cols = field.shape[1]
-    pairs, width = to_right.shape[0], to_right.shape[1] // 2
-    first = field.shape[0] - 2 * pairs
-    for p in range(pairs):
-        two = [field[first + 2 * p], field[first + 2 * p + 1]]
-        to_right[p] = jnp.concatenate([row[cols - width :] for row in two], 0)
-        to_left[p] = jnp.concatenate([row[:width] for row in two], 0)
-
-
-def unpack_edges(edges, low, high):
-    near_low, near_high, far_low, far_high = edges
-    near, halo, channels = near_low.shape[0], low.shape[1], low.shape[2]
-    pairs, width = far_low.shape[0], far_low.shape[1] // 2
-    blank = jnp.zeros((near, halo - NARROW, channels), low.dtype)
-    low[:near, : halo - NARROW] = blank
-    low[:near, halo - NARROW :] = near_low[...]
-    high[:near, :NARROW] = near_high[...]
-    high[:near, NARROW:] = blank
-    blank = jnp.zeros((halo - width, channels), low.dtype)
-    for p in range(pairs):
-        below, above = far_low[p], far_high[p]
-        for q in range(2):
-            cut = slice(q * width, (q + 1) * width)
-            low[near + 2 * p + q] = jnp.concatenate([blank, below[cut]], 0)
-            high[near + 2 * p + q] = jnp.concatenate([above[cut], blank], 0)
-
-
-def edge_copies(size, field, to_right, to_left, edges, sems):
+    begin, size, right, left = 0, 0, [], []
+    for i, width in enumerate(widths):
+        row = field[i]
+        right.append(row[cols - width :])
+        left.append(row[:width])
+        size += width
+        if i == len(widths) - 1 and size % 16:
+            blank = jnp.zeros((-size % 16, field.shape[2]), field.dtype)
+            right.append(blank)
+            left.append(blank)
+            size += blank.shape[0]
+        if size % 16 == 0:
+            to_right[begin : begin + size] = jnp.concatenate(right, 0)
+            to_left[begin : begin + size] = jnp.concatenate(left, 0)
+            begin, size, right, left = begin + size, 0, [], []
+
+
+def unpack_edges(widths, edges, low, high):
+    halo, channels = low.shape[1:]
+    start = 0
+    for i, width in enumerate(widths):
+        first, last = start // 16 * 16, -(-(start + width) // 16) * 16
+        cut = slice(start - first, start - first + width)
+        below, above = edges[0][first:last][cut], edges[1][first:last][cut]
+        blank = jnp.zeros((halo - width, channels), low.dtype)
+        low[i] = jnp.concatenate([blank, below], 0)
+        high[i] = jnp.concatenate([above, blank], 0)
+        start += width
+
+
+def edge_copies(size, to_right, to_left, edges, sems):
     right, left = sides(size)
-    near_low, near_high, far_low, far_high = edges
-    cols, near = field.shape[1], near_low.shape[0]
-    rows = pl.ds(0, near)
     return [
-        send(field.at[rows, pl.ds(cols - NARROW, NARROW)], near_low, sems.at[0], sems.at[1], right),
-        send(field.at[rows, pl.ds(0, NARROW)], near_high, sems.at[2], sems.at[3], left),
-        send(to_right, far_low, sems.at[4], sems.at[5], right),
-        send(to_left, far_high, sems.at[6], sems.at[7], left),
+        send(to_right, edges[0], sems.at[0], sems.at[1], right),
+        send(to_left, edges[1], sems.at[2], sems.at[3], left),
     ]
 
 
-def with_edges(size, body, at_field, at_edges, *refs):
+def with_edges(size, widths, body, at_field, at_edges, *refs):
     *refs, to_right, to_left, sems = refs
-    field, edges = refs[at_field], refs[at_edges : at_edges + 4]
+    field, edges = refs[at_field], refs[at_edges : at_edges + 2]
     step = pl.program_id(0)
 
     @pl.when(step == 0)
     def _():
-        pack_edges(field, to_right, to_left)
+        pack_edges(widths, field, to_right, to_left)
         greet(sides(size))
-        for copy in edge_copies(size, field, to_right, to_left, edges, sems):
+        for copy in edge_copies(size, to_right, to_left, edges, sems):
             copy.start()
 
-    body(*refs[:at_field], *refs[at_field + 1 : at_edges], *refs[at_edges + 4 :])
+    body(*refs[:at_field], *refs[at_field + 1 : at_edges], *refs[at_edges + 2 :])
 
     @pl.when(step == pl.num_programs(0) - 1)
     def _():
-        for copy in edge_copies(size, field, to_right, to_left, edges, sems):
+        for copy in edge_copies(size, to_right, to_left, edges, sems):
             copy.wait()
 
 
@@ -219,8 +221,7 @@
         full[pl.ds(pl.multiple_of(base2, 16), rp), :] = acc.astype(jnp.bfloat16)
 
     def finish():
-        total[0][...] = full[: rows // 2].astype(f32)
-        total[1][...] = full[rows // 2 :].astype(f32)
+        total[...] = full[...].astype(f32)
 
     waits = [[], halves, quarters, pieces, spreads, back1, back0]
     works = [None, add_half, add_quarter, add_pieces, None, None, finish]
@@ -252,7 +253,11 @@
 
 def run_stages(stages, step):
     for number, when in enumerate(SUM_STEPS, 1):
-        pl.when(step == when)(stages[number])
+
+        @pl.when(step == when)
+        def _():
+            for chain in stages:
+                chain[number]()
 
 
 def matrices_kernel(block, cols, ahead_ref, back_ref, ahead_out, back_out):
@@ -278,9 +283,9 @@
         grad_ref[...] += part
 
 
-def first_kernel(block, own, e0, e1, e2, e3, matrix, weight, pre_out, act_out, spread_out, low, high):
+def first_kernel(widths, block, own, e0, e1, matrix, weight, pre_out, act_out, spread_out, low, high):
     step = pl.program_id(0)
-    pl.when(step == 0)(lambda: unpack_edges((e0, e1, e2, e3), low, high))
+    pl.when(step == 0)(lambda: unpack_edges(widths, (e0, e1), low, high))
     spread_block(own, low, high, matrix, 0, spread_out, step * block, block)
     pre = jnp.dot(spread_out[...], weight[...], preferred_element_type=jnp.float32)
     pre_out[...] = pre
@@ -288,11 +293,11 @@
 
 
 def slope_kernel(
-    block, scale, own, e0, e1, e2, e3, matrix, weight, pre, spread_one, gp_out, grad_out,
+    widths, block, scale, own, e0, e1, matrix, weight, pre, spread_one, gp_out, grad_out,
     low, high, spread, grad,
 ):
     step = pl.program_id(0)
-    pl.when(step == 0)(lambda: unpack_edges((e0, e1, e2, e3), low, high))
+    pl.when(step == 0)(lambda: unpack_edges(widths, (e0, e1), low, high))
     spread_block(own, low, high, matrix, 0, spread, step * block, block)
     grad_act = jnp.dot(spread[...], weight[...], preferred_element_type=jnp.float32)
     gp = (grad_act * gelu_slope(pre[...])).astype(jnp.bfloat16)
@@ -305,11 +310,11 @@
 
 
 def second_kernel(
-    block, scale, own, e0, e1, e2, e3, matrix, weight, resid, cot, mixed_out, grad_out,
+    widths, block, scale, own, e0, e1, matrix, weight, resid, cot, mixed_out, grad_out,
     low, high, spread, grad,
 ):
     step = pl.program_id(0)
-    pl.when(step == 0)(lambda: unpack_edges((e0, e1, e2, e3), low, high))
+    pl.when(step == 0)(lambda: unpack_edges(widths, (e0, e1), low, high))
     spread_block(own, low, high, matrix, 0, spread, step * block, block)
     branch = jnp.dot(spread[...], weight[...], preferred_element_type=jnp.float32)
     flat = branch.shape
@@ -326,21 +331,22 @@
 
 
 def last_kernel(
-    size, block, own, e0, e1, e2, e3, matrix, weight, cot, grad_first, grad_second,
-    field_out, total_first, total_second, low, high, spread, local, *work
+    size, widths, block, own, e0, e1, matrix, weight, cot, grad_first, grad_second,
+    field_out, total_first, total_second, low, high, spread, *work
 ):
     step = pl.program_id(0)
-    *buffers, sum_sems = work
-    wide = grad_first.shape[0]
-    stages = sum_stages(size, local, buffers, (total_first, total_second), sum_sems)
+    half = len(work) // 2
+    stages = [
+        sum_stages(size, grad_first, work[: half - 1], total_first, work[half - 1]),
+        sum_stages(size, grad_second, work[half:-1], total_second, work[-1]),
+    ]
 
     @pl.when(step == 0)
     def _():
-        local[:wide] = grad_first[...]
-        local[wide:] = grad_second[...]
         greet(partners_of(size))
-        stages[0]()
-        unpack_edges((e0, e1, e2, e3), low, high)
+        for chain in stages:
+            chain[0]()
+        unpack_edges(widths, (e0, e1), low, high)
 
     run_stages(stages, step)
     spread_block(own, low, high, matrix, 0, spread, step * block, block)
@@ -353,7 +359,8 @@
 
     @pl.when(step == pl.num_programs(0) - 1)
     def _():
-        stages[-1]()
+        for chain in stages:
+            chain[-1]()
 
 
 def on_device(
@@ -378,11 +385,8 @@
     field_spec = by_row((block, cols, channels))
     matrix_spec = by_row((block, kernels * cols, 3 * LANES))
     bands = support.shape[0]
-    wider = [b for b in range(bands) if (cols // 2) * (b + 1) // bands > NARROW]
-    near = max((min(wider) * (rows // bands) - 1) // 2 * 2, 2)
-    near_shape = (near, NARROW, channels)
-    far_shape = ((rows - near) // 2, 2 * (cols // 2), channels)
-    edge_shapes = [near_shape, near_shape, far_shape, far_shape]
+    widths = edge_widths(rows, bands, cols // 2)
+    edge_shapes = [(-(-sum(widths) // 16) * 16, channels)] * 2
     common = (
         [whole((rows, cols, channels))]
         + [whole(shape) for shape in edge_shapes]
@@ -411,26 +415,26 @@
     unpacked = [pltpu.VMEM((rows, halo, channels), bf16)] * 2
     total_type = jax.ShapeDtypeStruct((wide, channels), f32)
     anywhere = pl.BlockSpec(memory_space=pl.ANY)
-    edge_work = [pltpu.VMEM(far_shape, bf16)] * 2 + [pltpu.SemaphoreType.DMA((8,))]
+    edge_work = [pltpu.VMEM(shape, bf16) for shape in edge_shapes] + [pltpu.SemaphoreType.DMA((4,))]
     table_spec = by_row((block, kernels * 3, LANES))
     edged = lambda body, at_field, at_edges: functools.partial(
-        with_edges, size, body, at_field, at_edges
+        with_edges, size, widths, body, at_field, at_edges
     )
     m_ahead, m_back, *act_edges = call(
         0,
         edged(functools.partial(matrices_kernel, block, cols), 2, 5),
         in_specs=[table_spec, table_spec, field_whole],
-        out_specs=[matrix_spec, matrix_spec] + [anywhere] * 4,
+        out_specs=[matrix_spec, matrix_spec] + [anywhere] * 2,
         out_shape=[matrix_type, matrix_type] + edge_types,
         scratch_shapes=edge_work,
     )(ahead, back, activations)
     cells = rows * cols
     pre, activated, spread_one, *cot_edges = call(
         1,
-        edged(functools.partial(first_kernel, block), 7, 11),
+        edged(functools.partial(first_kernel, widths, block), 5, 9),
         in_specs=common + [field_whole],
         out_specs=[by_row((block * cols, channels)), field_spec, by_row(spread_shape)]
-        + [anywhere] * 4,
+        + [anywhere] * 2,
         out_shape=[
             jax.ShapeDtypeStruct((cells, channels), f32),
             field_type,
@@ -441,31 +445,30 @@
     )(activations, *act_edges, m_ahead, flat_first, cotangent)
     gp, grad_first, *mid_edges = call(
         2,
-        edged(functools.partial(slope_kernel, block, scale), 9, 12),
+        edged(functools.partial(slope_kernel, widths, block, scale), 7, 10),
         in_specs=common + [by_row((block * cols, channels)), by_row(spread_shape), field_whole],
-        out_specs=[field_spec, whole((wide, channels))] + [anywhere] * 4,
+        out_specs=[field_spec, whole((wide, channels))] + [anywhere] * 2,
         out_shape=[field_type, grad_type] + edge_types,
         scratch_shapes=unpacked + work + edge_work,
     )(cotangent, *cot_edges, m_back, turned_second, pre, spread_one, activated)
     mixed, grad_second, *gp_edges = call(
         3,
-        edged(functools.partial(second_kernel, block, scale), 9, 12),
+        edged(functools.partial(second_kernel, widths, block, scale), 7, 10),
         in_specs=common + [field_spec, field_spec, field_whole],
-        out_specs=[field_spec, whole((wide, channels))] + [anywhere] * 4,
+        out_specs=[field_spec, whole((wide, channels))] + [anywhere] * 2,
         out_shape=[field_type, grad_type] + edge_types,
         scratch_shapes=unpacked + work + edge_work,
     )(activated, *mid_edges, m_ahead, flat_second, activations, cotangent, gp)
     grad_spec = whole((wide, channels))
     grad_field, total_first, total_second = call(
         4,
-        functools.partial(last_kernel, size, block),
+        functools.partial(last_kernel, size, widths, block),
         in_specs=common + [field_spec, grad_spec, grad_spec],
         out_specs=[field_spec, grad_spec, grad_spec],
         out_shape=[field_type, total_type, total_type],
         scratch_shapes=unpacked
         + work[:1]
-        + [pltpu.VMEM((2 * wide, channels), bf16)]
-        + sum_scratch(2 * wide, channels, size),
+        + sum_scratch(wide, channels, size) * 2,
     )(gp, *gp_edges, m_back, turned_first, cotangent, grad_first, grad_second)
     return (
         mixed,

time: 140 us -> 122 us (0.87)
  Pallas kernels: 124 us -> 106 us
    pallas_call x4, Pallas kernels: 105 us -> 87.7 us  [the longest x1 31 us: on_device(): call(4, functools.partial(last_kernel, size, widths, block), in_specs=com...]
where the time goes in v3:
time: 122 us; the launch traced here: 121 us
  Pallas kernels  106 us (87%)
  local copies, waits for them, and re-layouts  10.7 us (9%)
  other arithmetic  2.56 us (2%)
    pallas_call x1, Pallas kernels, on_device(): call(4, functools.partial(last_kernel, size, widths, block), in_specs=com...  31 us
    pallas_call x1, Pallas kernels, on_device(): call(2, edged(functools.partial(slope_kernel, widths, block, scale), 7, 1...  21 us
    pallas_call x1, Pallas kernels, on_device(): call(3, edged(functools.partial(second_kernel, widths, block, scale), 7,...  19.5 us
    pallas_call x1, Pallas kernels, on_device(): call(0, edged(functools.partial(matrices_kernel, block, cols), 2, 5), in_...  18.7 us
    pallas_call x1, Pallas kernels, on_device(): call(1, edged(functools.partial(first_kernel, widths, block), 5, 9), in_s...  16.2 us
    unnamed x16, local copies, waits for them, and re-layouts  6.35 us

profile of v3, /device:TPU:0, one launch (start us, length us, event | category | flops | bytes accessed | tf_op | source)
XLA Modules:
  0.0 121.0 jit_solution(8966503036507121802)
XLA Ops:
  0.6 0.9 reshape.83
  1.6 0.2 copy.17
  1.8 0.7 multiply_add_fusion
  2.4 0.7 iota_compare_fusion.2
  3.2 0.3 convolution_bitcast_fusion
  3.6 1.0 copy.22.refs_1_
  4.6 0.3 convolution_bitcast_fusion.1
  4.9 0.1 copy.16
  5.0 1.1 copy_select_fusion.refs_0_
  6.2 18.7 %shard_map.102 = (bf16[64,192,384]{2,1,0:T(8,128)(2,1)}, bf16[64,192,384]{2,1,0:T(8,128)(2,1)}, bf16[1040,256]{1,0:T(8,128)(2,1)}, bf16[1040,256]{1,0:T(8,128)(2,1)}) custom-call(f32[64,12,128]{2,1,0:T(8,128)} %copy_select_fusion.refs_0_, f32[64,12,128]{2,1,0:T(8,128)} %copy.22.refs_1_, bf16[64,48,256]{2,1,0:T(8,128)(2,1)} %refs_5_.3), custom_call_target="tpu_custom_call" | custom-call | tf_op jit(solution)/shard_map/pallas_call | solution.py:423
  24.9 0.0 copy-start
  24.9 16.2 %shard_map.103 = (f32[3072,256]{1,0:T(8,128)}, bf16[64,48,256]{2,1,0:T(8,128)(2,1)}, bf16[3072,1024]{1,0:T(8,128)(2,1)}, bf16[1040,256]{1,0:T(8,128)(2,1)}, bf16[1040,256]{1,0:T(8,128)(2,1)}) custom-call(bf16[64,48,256]{2,1,0:T(8,128)(2,1)} %refs_5_.3, bf16[1040,256]{1,0:T(8,128)(2,1)} %get-tuple-element.24.refs_1_, ...), custom_call_target="tpu_custom_call" | custom-call | tf_op jit(solution)/shard_map/pallas_call | solution.py:432
  41.1 0.0 copy-done
  41.1 1.0 copy.23
  42.1 21.0 %shard_map.104 = (bf16[64,48,256]{2,1,0:T(8,128)(2,1)}, bf16[1024,256]{1,0:T(8,128)(2,1)}, bf16[1040,256]{1,0:T(8,128)(2,1)}, bf16[1040,256]{1,0:T(8,128)(2,1)}) custom-call(bf16[64,48,256]{2,1,0:T(8,128)(2,1)} %cot.1, bf16[1040,256]{1,0:T(8,128)(2,1)} %get-tuple-element.28.refs_1_, bf16[1040,256]{1,0:T(8,128)(2,1)} %get-tuple-element.29.refs_2_, ...), custom_call_target="tpu_custom_call" | custom-call | tf_op jit(solution)/shard_map/pallas_call | solution.py:446
  63.1 0.0 copy-start.1
  63.1 19.5 %shard_map.105 = (bf16[64,48,256]{2,1,0:T(8,128)(2,1)}, bf16[1024,256]{1,0:T(8,128)(2,1)}, bf16[1040,256]{1,0:T(8,128)(2,1)}, bf16[1040,256]{1,0:T(8,128)(2,1)}) custom-call(bf16[64,48,256]{2,1,0:T(8,128)(2,1)} %get-tuple-element.27.refs_7_.refs_0_, bf16[1040,256]{1,0:T(8,128)(2,1)} %get-tuple-element.33.refs_1_, ...), custom_call_target="tpu_custom_call" | custom-call | tf_op jit(solution)/shard_map/pallas_call | solution.py:454
  82.7 0.0 copy-done.1
  82.7 1.0 copy.24
  83.7 0.0 copy-start.2
  83.7 31.0 %shard_map.106 = (bf16[64,48,256]{2,1,0:T(8,128)(2,1)}, f32[1024,256]{1,0:T(8,128)}, f32[1024,256]{1,0:T(8,128)}) custom-call(bf16[64,48,256]{2,1,0:T(8,128)(2,1)} %get-tuple-element.35.refs_7_.own, bf16[1040,256]{1,0:T(8,128)(2,1)} %get-tuple-element.37.e0, bf16[1040,256]{1,0:T(8,128)(2,1)} %get-tuple-element.38.e1, ...), custom_call_target="tpu_custom_call" | custom-call | tf_op jit(solution)/shard_map/pallas_call | solution.py:463
  114.7 0.0 copy-done.2
  114.7 0.0 copy-start.3
  114.7 1.1 copy.32
  115.8 0.8 copy-done.3
  116.7 0.0 copy-start.5
  116.7 1.1 copy.33
  117.8 0.6 copy-done.5
  118.4 0.0 copy-start.4
  118.4 1.0 copy.34
  119.4 0.6 copy-done.4
  120.0 1.0 copy.35
  (7 shorter events, 0.2 us)
Async XLA Ops:
  24.9 16.2 %copy-start = (bf16[4,256,256]{2,1,0:T(8,128)(2,1)S(1)}, bf16[4,256,256]{2,1,0:T(8,128)(2,1)}, u32[]{:S(2)}) copy-start(bf16[4,256,256]{2,1,0:T(8,128)(2,1)} %param.12) | copy-start | bytes 1572868
  63.1 19.6 %copy-start.1 = (bf16[4,256,256]{2,1,0:T(8,128)(2,1)S(1)}, bf16[4,256,256]{2,1,0:T(8,128)(2,1)}, u32[]{:S(2)}) copy-start(bf16[4,256,256]{2,1,0:T(8,128)(2,1)} %param.11) | copy-start | bytes 1572868
  83.7 31.0 %copy-start.2 = (bf16[64,48,256]{2,1,0:T(8,128)(2,1)S(1)}, bf16[64,48,256]{2,1,0:T(8,128)(2,1)}, u32[]{:S(2)}) copy-start(bf16[64,48,256]{2,1,0:T(8,128)(2,1)} %get-tuple-element.53) | copy-start | bytes 4718596
  114.7 2.0 %copy-start.3 = (bf16[64,48,256]{2,1,0:T(8,128)(2,1)S(1)}, bf16[64,48,256]{2,1,0:T(8,128)(2,1)}, u32[]{:S(2)}) copy-start(bf16[64,48,256]{2,1,0:T(8,128)(2,1)} %get-tuple-element.54) | copy-start | bytes 4718596
  116.7 1.8 %copy-start.5 = (f32[1024,256]{1,0:T(8,128)S(1)}, f32[1024,256]{1,0:T(8,128)}, u32[]{:S(2)}) copy-start(f32[1024,256]{1,0:T(8,128)} %get-tuple-element.42) | copy-start | bytes 3145732
  118.4 1.6 %copy-start.4 = (f32[1024,256]{1,0:T(8,128)S(1)}, f32[1024,256]{1,0:T(8,128)}, u32[]{:S(2)}) copy-start(f32[1024,256]{1,0:T(8,128)} %get-tuple-element.43) | copy-start | bytes 3145732

commit v4 on v3

--- a/solution.py
+++ b/solution.py
@@ -9,7 +9,7 @@
 from jax.sharding import PartitionSpec as P
 
 LANES = 128
-GRAIN = 4
+GRAIN = 2
 VMEM_LIMIT = 56 * 1024 * 1024
 
 
@@ -335,11 +335,13 @@
     field_out, total_first, total_second, low, high, spread, *work
 ):
     step = pl.program_id(0)
-    half = len(work) // 2
-    stages = [
-        sum_stages(size, grad_first, work[: half - 1], total_first, work[half - 1]),
-        sum_stages(size, grad_second, work[half:-1], total_second, work[-1]),
-    ]
+    each, rows = len(work) // 4, grad_first.shape[0] // 2
+    stages = []
+    for number in range(4):
+        cut = pl.ds(number // 2 * rows, rows)
+        grad, total = ((grad_first, total_first), (grad_second, total_second))[number % 2]
+        *buffers, sems = work[number * each : (number + 1) * each]
+        stages.append(sum_stages(size, grad.at[cut], buffers, total.at[cut], sems))
 
     @pl.when(step == 0)
     def _():
@@ -468,7 +470,7 @@
         out_shape=[field_type, total_type, total_type],
         scratch_shapes=unpacked
         + work[:1]
-        + sum_scratch(wide, channels, size) * 2,
+        + sum_scratch(wide // 2, channels, size) * 4,
     )(gp, *gp_edges, m_back, turned_first, cotangent, grad_first, grad_second)
     return (
         mixed,

time: 122 us -> 120 us (0.984)
  Pallas kernels: 106 us -> 104 us
    pallas_call x1, Pallas kernels: 31 us -> 29.5 us  [on_device(): call(4, functools.partial(last_kernel, size, widths, block), in_specs=com...]
where the time goes in v4:
time: 120 us; the launch traced here: 119 us
  Pallas kernels  104 us (87%)
  local copies, waits for them, and re-layouts  10.7 us (9%)
  other arithmetic  2.56 us (2%)
    pallas_call x1, Pallas kernels, on_device(): call(4, functools.partial(last_kernel, size, widths, block), in_specs=com...  29.5 us
    pallas_call x1, Pallas kernels, on_device(): call(2, edged(functools.partial(slope_kernel, widths, block, scale), 7, 1...  21.4 us
    pallas_call x1, Pallas kernels, on_device(): call(3, edged(functools.partial(second_kernel, widths, block, scale), 7,...  19.2 us
    pallas_call x1, Pallas kernels, on_device(): call(0, edged(functools.partial(matrices_kernel, block, cols), 2, 5), in_...  18.8 us
    pallas_call x1, Pallas kernels, on_device(): call(1, edged(functools.partial(first_kernel, widths, block), 5, 9), in_s...  15.5 us
    unnamed x16, local copies, waits for them, and re-layouts  6.35 us

profile of v4, /device:TPU:0, one launch (start us, length us, event | category | flops | bytes accessed | tf_op | source)
XLA Modules:
  0.0 119.0 jit_solution(11205632802207787087)
XLA Ops:
  0.6 0.9 reshape.83
  1.6 0.2 copy.17
  1.8 0.7 multiply_add_fusion
  2.4 0.7 iota_compare_fusion.2
  3.2 0.3 convolution_bitcast_fusion
  3.6 1.0 copy.22.refs_1_
  4.6 0.3 convolution_bitcast_fusion.1
  4.9 0.1 copy.16
  5.0 1.1 copy_select_fusion.refs_0_
  6.2 18.8 %shard_map.102 = (bf16[64,192,384]{2,1,0:T(8,128)(2,1)}, bf16[64,192,384]{2,1,0:T(8,128)(2,1)}, bf16[992,256]{1,0:T(8,128)(2,1)}, bf16[992,256]{1,0:T(8,128)(2,1)}) custom-call(f32[64,12,128]{2,1,0:T(8,128)} %copy_select_fusion.refs_0_, f32[64,12,128]{2,1,0:T(8,128)} %copy.22.refs_1_, bf16[64,48,256]{2,1,0:T(8,128)(2,1)} %refs_5_.3), custom_call_target="tpu_custom_call" | custom-call | tf_op jit(solution)/shard_map/pallas_call | solution.py:425
  25.0 0.0 copy-start
  25.0 15.5 %shard_map.103 = (f32[3072,256]{1,0:T(8,128)}, bf16[64,48,256]{2,1,0:T(8,128)(2,1)}, bf16[3072,1024]{1,0:T(8,128)(2,1)}, bf16[992,256]{1,0:T(8,128)(2,1)}, bf16[992,256]{1,0:T(8,128)(2,1)}) custom-call(bf16[64,48,256]{2,1,0:T(8,128)(2,1)} %refs_5_.3, bf16[992,256]{1,0:T(8,128)(2,1)} %get-tuple-element.24.refs_1_, ...), custom_call_target="tpu_custom_call" | custom-call | tf_op jit(solution)/shard_map/pallas_call | solution.py:434
  40.4 0.0 copy-done
  40.4 1.0 copy.23
  41.4 21.4 %shard_map.104 = (bf16[64,48,256]{2,1,0:T(8,128)(2,1)}, bf16[1024,256]{1,0:T(8,128)(2,1)}, bf16[992,256]{1,0:T(8,128)(2,1)}, bf16[992,256]{1,0:T(8,128)(2,1)}) custom-call(bf16[64,48,256]{2,1,0:T(8,128)(2,1)} %cot.1, bf16[992,256]{1,0:T(8,128)(2,1)} %get-tuple-element.28.refs_1_, bf16[992,256]{1,0:T(8,128)(2,1)} %get-tuple-element.29.refs_2_, ...), custom_call_target="tpu_custom_call" | custom-call | tf_op jit(solution)/shard_map/pallas_call | solution.py:448
  62.9 0.0 copy-start.1
  62.9 19.2 %shard_map.105 = (bf16[64,48,256]{2,1,0:T(8,128)(2,1)}, bf16[1024,256]{1,0:T(8,128)(2,1)}, bf16[992,256]{1,0:T(8,128)(2,1)}, bf16[992,256]{1,0:T(8,128)(2,1)}) custom-call(bf16[64,48,256]{2,1,0:T(8,128)(2,1)} %get-tuple-element.27.refs_7_.refs_0_, bf16[992,256]{1,0:T(8,128)(2,1)} %get-tuple-element.33.refs_1_, bf16[992,256]{1,0:T(8,128)(2,1)} %get-tuple-element.34.refs_2_, ...), custom_call_target="tpu_custom_call" | custom-call | tf_op jit(solution)/shard_map/pallas_call | solution.py:456
  82.1 0.0 copy-done.1
  82.1 1.0 copy.24
  83.1 0.0 copy-start.2
  83.1 29.5 %shard_map.106 = (bf16[64,48,256]{2,1,0:T(8,128)(2,1)}, f32[1024,256]{1,0:T(8,128)}, f32[1024,256]{1,0:T(8,128)}) custom-call(bf16[64,48,256]{2,1,0:T(8,128)(2,1)} %get-tuple-element.35.refs_7_.own, bf16[992,256]{1,0:T(8,128)(2,1)} %get-tuple-element.37.e0, bf16[992,256]{1,0:T(8,128)(2,1)} %get-tuple-element.38.e1, ...), custom_call_target="tpu_custom_call" | custom-call | tf_op jit(solution)/shard_map/pallas_call | solution.py:465
  112.6 0.0 copy-done.2
  112.6 0.0 copy-start.3
  112.6 1.1 copy.32
  113.8 0.8 copy-done.3
  114.6 0.0 copy-start.5
  114.6 1.1 copy.33
  115.7 0.6 copy-done.5
  116.4 0.0 copy-start.4
  116.4 1.0 copy.34
  117.4 0.6 copy-done.4
  118.0 1.0 copy.35
  (7 shorter events, 0.2 us)
Async XLA Ops:
  25.0 15.5 %copy-start = (bf16[4,256,256]{2,1,0:T(8,128)(2,1)S(1)}, bf16[4,256,256]{2,1,0:T(8,128)(2,1)}, u32[]{:S(2)}) copy-start(bf16[4,256,256]{2,1,0:T(8,128)(2,1)} %param.12) | copy-start | bytes 1572868
  62.9 19.2 %copy-start.1 = (bf16[4,256,256]{2,1,0:T(8,128)(2,1)S(1)}, bf16[4,256,256]{2,1,0:T(8,128)(2,1)}, u32[]{:S(2)}) copy-start(bf16[4,256,256]{2,1,0:T(8,128)(2,1)} %param.11) | copy-start | bytes 1572868
  83.1 29.5 %copy-start.2 = (bf16[64,48,256]{2,1,0:T(8,128)(2,1)S(1)}, bf16[64,48,256]{2,1,0:T(8,128)(2,1)}, u32[]{:S(2)}) copy-start(bf16[64,48,256]{2,1,0:T(8,128)(2,1)} %get-tuple-element.53) | copy-start | bytes 4718596
  112.6 2.0 %copy-start.3 = (bf16[64,48,256]{2,1,0:T(8,128)(2,1)S(1)}, bf16[64,48,256]{2,1,0:T(8,128)(2,1)}, u32[]{:S(2)}) copy-start(bf16[64,48,256]{2,1,0:T(8,128)(2,1)} %get-tuple-element.54) | copy-start | bytes 4718596
  114.6 1.8 %copy-start.5 = (f32[1024,256]{1,0:T(8,128)S(1)}, f32[1024,256]{1,0:T(8,128)}, u32[]{:S(2)}) copy-start(f32[1024,256]{1,0:T(8,128)} %get-tuple-element.42) | copy-start | bytes 3145732
  116.4 1.6 %copy-start.4 = (f32[1024,256]{1,0:T(8,128)S(1)}, f32[1024,256]{1,0:T(8,128)}, u32[]{:S(2)}) copy-start(f32[1024,256]{1,0:T(8,128)} %get-tuple-element.43) | copy-start | bytes 3145732
